TPU v7x, 128 devices: a whole 4x4x4 slice. The times are simulated.
128 devices in a mesh: slide: 8 (over x, core), enc: 16 (over y, z).
Axes of the slice: x: 4, y: 4, z: 4, core: 2. Of those that a mesh axis runs over, the one named last changes fastest.
Arguments:
- tile_maps: bfloat16 [8, 512, 7, 7, 768], P('slide', 'enc'), may hold values from -6 to 6
- tile_owner: int32 [8, 512, 1], P('slide', 'enc'), may hold values from 0 to 15; in each aligned block of 32 rows (0 to 31, 32 to 63, ..., all dimensions but the last counted through in order) at most 3 rows name the same one
- tissue_counts: int32 [8, 16], P('slide'), may hold values from 1 to 32, as said below
- embed_grad: bfloat16 [8, 16, 16, 3, 768], P('slide', 'enc'), may hold values from -1.5 to 1.5
- depth_kernel: bfloat16 [7, 7, 768], replicated, may hold values from -0.875 to 0.875
- up_weight: bfloat16 [3072, 768], replicated, may hold values from -0.21875 to 0.21875
- down_weight: bfloat16 [3072, 768], replicated, may hold values from -0.109375 to 0.109375
Outputs:
- slide_embed: bfloat16 [8, 16, 16, 3, 768], P('slide', 'enc')
- up_grad: float32 [3072, 768], P(('slide', 'enc'))
- down_grad: float32 [3072, 768], P(('slide', 'enc'))
Inputs may be any that keep to these rules, and one draw needn't show every extreme that they name: `tissue_counts`: within one slide row, a reader's count plus the count of the reader half the enc axis away is at most 48; some pair reaches it. `tile_owner`: among the 32 slots of one reader no owner is named more than 3 times; some reader reaches it.
All inputs are finite; a program needn't handle non-finite values.
Results may differ from a plain program's by a relative error of at most 0.015.
Values may be sent and summed in bfloat16 or wider, within the bound.
No kernel may reach another device: no remote copies, remote signals or barrier semaphores. Data moves between devices by JAX's collectives and lax.ppermute only.
A program may use at most 256 MiB of HBM per device.

v0:
```python
import functools

import jax
import jax.numpy as jnp
from jax import lax
from jax.experimental import pallas as pl
from jax.experimental.pallas import tpu as pltpu
from jax.sharding import PartitionSpec as P

root_half = 0.7071067811865476
half_log2_e = -0.7213475204444817
log2_inv_root_two_pi = -1.3257480647361592
axes = ("slide", "enc")
hops = (2, 1, 3)
VMEM = pl.BlockSpec(memory_space=pltpu.VMEM)
SMEM = pl.BlockSpec(memory_space=pltpu.SMEM)
HBM = pl.BlockSpec(memory_space=pltpu.HBM)
small_cost = pl.CostEstimate(flops=1000, bytes_accessed=1000, transcendentals=0)
nt = (((1,), (1,)), ((), ()))
tn = (((0,), (0,)), ((), ()))


def f32_dot(lhs, rhs, dims=(((1,), (0,)), ((), ()))):
    return lax.dot_general(lhs, rhs, dims, preferred_element_type=jnp.float32)


def row_hits(index, size):
    return index == lax.broadcasted_iota(jnp.int32, (index.shape[0], size), 1)


def slot_tables(counts_ref, owners_ref, table_ref, send_ref, place_ref):
    enc = lax.axis_index("enc")
    count, y, z = counts_ref[0, enc], enc // 4, enc % 4
    lanes, tiles = counts_ref.shape[1], owners_ref.shape[1]
    slot = lax.broadcasted_iota(jnp.int32, (tiles, tiles), 0)
    other = lax.broadcasted_iota(jnp.int32, (tiles, tiles), 1)
    line = jnp.broadcast_to(owners_ref[...], (tiles, tiles)).astype(jnp.float32)
    owners = jnp.sum(jnp.where(slot == other, line, 0.0), axis=1, keepdims=True)
    same = jnp.where((owners == line) & (other < slot), 1.0, 0.0)
    owners = owners.astype(jnp.int32)
    rank = jnp.sum(same, axis=1, keepdims=True).astype(jnp.int32)
    live = lax.broadcasted_iota(jnp.int32, (tiles, 1), 0) < count
    pick = lambda index, size, on: jnp.where(row_hits(index, size) & on, 1.0, 0.0).astype(jnp.bfloat16)
    table_ref[...] = pick(rank * lanes + owners, table_ref.shape[1], live)
    hops_y, hops_z = ((owners >> 2) - y) & 3, ((owners & 3) - z) & 3
    send_ref[...] = pick(hops_y * 16 + hops_z * 3 + rank, send_ref.shape[1], live)
    spots = lax.broadcasted_iota(jnp.int32, (place_ref.shape[0], 1), 0)
    reader = spots & (lanes - 1)
    from_y, from_z = (y - (reader >> 2)) & 3, (z - (reader & 3)) & 3
    place_ref[...] = pick(from_z * 16 + from_y * 3 + (spots >> 4), place_ref.shape[1], spots >= 0)


def conv_kernel(counts_ref, owners_ref, x_hbm, k_hbm, up_hbm, down_hbm, *rest):
    normed_ref, mean_ref, table_ref, send_ref, place_ref = rest[0:5]
    weights = rest[5:13]
    xb, kb, xf, kf, cv, sems = rest[13:]
    side = kb.shape[0]
    tiles, width = mean_ref.shape
    cells, reach = side * side, side // 2
    units = weights[0].shape[0]
    sub = units // 4
    slide, enc = lax.axis_index("slide"), lax.axis_index("enc")
    x, core, y = slide // 2, slide % 2, enc // 4
    first = jnp.where(core == 0, x, y)
    second = jnp.where(core == 0, y, x)

    def maps_copy(group):
        rows = pl.ds(group * 16, 16)
        return pltpu.make_async_copy(x_hbm.at[:, :, rows, :], xb.at[group], sems.at[group])

    def weight_copy(n):
        goal = lax.rem(first + (hops + (0,))[n % 16 // 4], 4)
        inner = lax.rem(second + n % 4 + 1, 4)
        row = jnp.where(core == 0, 8 * goal + inner, 8 * inner + goal) + 4 * core
        start = pl.ds(pl.multiple_of(row * sub, sub), sub)
        source = (up_hbm if n < 16 else down_hbm).at[start, :]
        goal = weights[n // 4].at[pl.ds(n % 4 * sub, sub), :]
        return pltpu.make_async_copy(source, goal, sems.at[3 + n])

    kernel_copy = pltpu.make_async_copy(k_hbm, kb, sems.at[2])
    kernel_copy.start()
    for group in range(tiles // 16):
        maps_copy(group).start()
    for n in range(32):
        weight_copy(n).start()
    slot_tables(counts_ref, owners_ref, table_ref, send_ref, place_ref)
    kernel_copy.wait()
    for n in range(cells):
        kf[n] = jnp.broadcast_to(
            kb[n // side, n % side : n % side + 1].astype(jnp.float32), (8, width)
        )

    @pl.loop(0, tiles // 16)
    def _(group):
        row = pl.multiple_of(group * 16, 16)
        maps_copy(group).wait()
        for n in range(cells):
            xf[n] = xb[group, n // side, n % side].astype(jnp.float32)

        @pl.loop(0, 2 * (width // 128))
        def _(unit):
            lane = pl.multiple_of((unit // 2) * 128, 128)
            half = pl.multiple_of((unit % 2) * 8, 8)
            for i in range(side):
                acc = [None] * side
                for a in range(side):
                    r = i + a - reach
                    if not 0 <= r < side:
                        continue
                    xs = [xf[r * side + j, pl.ds(half, 8), pl.ds(lane, 128)] for j in range(side)]
                    ks = [kf[a * side + b, :, pl.ds(lane, 128)] for b in range(side)]
                    for j in range(side):
                        for b in range(side):
                            c = j + b - reach
                            if 0 <= c < side:
                                term = xs[c] * ks[b]
                                acc[j] = term if acc[j] is None else acc[j] + term
                for j in range(side):
                    cv[i * side + j, pl.ds(half, 8), pl.ds(lane, 128)] = acc[j]

        total = None
        for n in range(cells):
            conv = cv[n]
            centred = conv - jnp.sum(conv, axis=1, keepdims=True) * (1.0 / width)
            var = jnp.sum(centred * centred, axis=1, keepdims=True) * (1.0 / width)
            normed_ref[n, pl.ds(row, 16), :] = (centred * lax.rsqrt(var + 1e-6)).astype(jnp.bfloat16)
            total = xf[n] if total is None else total + xf[n]
        mean_ref[pl.ds(row, 16), :] = total * (1.0 / cells)

    for n in range(32):
        weight_copy(n).wait()


def conv_norm(counts, owners, maps, kernel, up_weight, down_weight, capacity):
    side, _, tiles, width = maps.shape
    cells = side * side
    units = up_weight.shape[0] // 8
    shape = jax.ShapeDtypeStruct
    return pl.pallas_call(
        conv_kernel,
        out_shape=(
            shape((cells, tiles, width), jnp.bfloat16),
            shape((tiles, width), jnp.float32),
            shape((tiles, 16 * capacity), jnp.bfloat16),
            shape((tiles, 64), jnp.bfloat16),
            shape((16 * capacity, 64), jnp.bfloat16),
            *[shape((units, width), jnp.bfloat16)] * 8,
        ),
        in_specs=[SMEM, VMEM] + [HBM] * 4,
        out_specs=(VMEM,) * 13,
        scratch_shapes=[
            pltpu.VMEM((tiles // 16, side, side, 16, width), jnp.bfloat16),
            pltpu.VMEM(kernel.shape, jnp.bfloat16),
            pltpu.VMEM((cells, 16, width), jnp.float32),
            pltpu.VMEM((cells, 8, width), jnp.float32),
            pltpu.VMEM((cells, 16, width), jnp.float32),
            pltpu.SemaphoreType.DMA((35,)),
        ],
        compiler_params=pltpu.CompilerParams(vmem_limit_bytes=46 << 20),
        cost_estimate=small_cost,
        name="conv_norm",
    )(counts, owners.reshape(1, tiles), maps, kernel, up_weight, down_weight)


def gelu_pair(pre):
    cdf = 0.5 + 0.5 * lax.erf(pre * root_half)
    density = jnp.exp2(pre * pre * half_log2_e + log2_inv_root_two_pi)
    return pre * cdf, cdf + pre * density


def block_kernel(*rest):
    parts, sgs = rest[0:2], rest[2:4]
    up_s, dn_s, emb_ref, pay_ref, emb_out, grads = rest[4:]
    units = up_s.shape[0]
    tiles = sgs[0].shape[0]
    scale = 1.0 / (parts[0].shape[0] // tiles)
    up = up_s[...]
    both = jnp.concatenate([sg[...] for sg in sgs for _ in range(128 // tiles)], axis=0)
    dh_both = f32_dot(dn_s[...], both, nt) * scale
    dh = [dh_both[:, 0:128], dh_both[:, 128:256]]

    runs, tails = [], []
    for p, ref in enumerate(parts):
        full = ref.shape[0] // 256 * 256
        runs.append((p, full))
        for cut in range(full, ref.shape[0], 128):
            tails.append((p, cut, min(128, ref.shape[0] - cut)))
    tails.sort(key=lambda t: -t[2])
    pool = [jnp.zeros((units, 128), jnp.float32) for _ in range(2)]
    column = 0

    def tile(rhs, owners, column):
        pre = f32_dot(up, rhs, nt)
        at = 0
        for who, w in owners:
            hid, slope = gelu_pair(pre[:, at : at + w])
            grads[:, column + at : column + at + w] = (slope * dh[who][:, 0:w]).astype(jnp.bfloat16)
            if w < 128:
                hid = jnp.concatenate([hid, jnp.zeros((units, 128 - w), jnp.float32)], axis=1)
            pool[who] = pool[who] + hid
            at += w

    up_rows, waiting = None, None

    def absorb(todo, up_rows):
        start, size, rhs = todo
        term = f32_dot(grads[:, start : start + size], rhs())
        return term if up_rows is None else up_rows + term

    for p, full in runs:
        start = column
        for cut in range(0, full, 256):
            tile(parts[p][cut : cut + 256, :], [(p, 128)] * 2, column)
            column += 256
        if waiting is not None:
            up_rows = absorb(waiting, up_rows)
        waiting = (start, full, lambda p=p, full=full: parts[p][0:full, :])
    start = column
    group, size = [], 0
    for n, (p, cut, w) in enumerate(tails):
        group.append((p, cut, w))
        size += w
        if size == 256 or n == len(tails) - 1:
            rhs = jnp.concatenate([parts[q][c : c + v, :] for q, c, v in group], axis=0)
            tile(rhs, [(q, v) for q, _, v in group], column)
            column += size
            group, size = [], 0
    up_rows = absorb(waiting, up_rows)
    rhs = jnp.concatenate([parts[p][c : c + w, :] for p, c, w in tails], axis=0)
    up_rows = absorb((start, column - start, lambda: rhs), up_rows)
    pay_ref[0:units] = up_rows.astype(jnp.bfloat16)

    pick = (
        lax.broadcasted_iota(jnp.int32, (tiles, 128), 0)
        == lax.broadcasted_iota(jnp.int32, (tiles, 128), 1)
    ).astype(jnp.bfloat16)
    flat = []
    for value in pool:
        shift = 64
        while shift >= tiles:
            value = value + pltpu.roll(value, shift, 1)
            shift //= 2
        flat.append(f32_dot(pick, (value * scale).astype(jnp.bfloat16), nt).astype(jnp.bfloat16))
    emb_out[...] = emb_ref[...] + f32_dot(jnp.concatenate(flat, axis=0), dn_s[...])
    for h in range(2):
        pay_ref[units + h * tiles : units + (h + 1) * tiles] = sgs[h][...]
        pay_ref[units + 2 * tiles : units + 3 * tiles, h * units : (h + 1) * units] = flat[h]


def hidden_block(parts, grads, up, down, emb):
    tiles, width = grads[0].shape
    units = up.shape[0]
    rows = sum(p.shape[0] for p in parts)
    return pl.pallas_call(
        block_kernel,
        out_shape=(
            jax.ShapeDtypeStruct((units + 3 * tiles, width), jnp.bfloat16),
            jax.ShapeDtypeStruct((2 * tiles, width), jnp.float32),
        ),
        in_specs=[VMEM] * 7,
        out_specs=(VMEM, VMEM),
        scratch_shapes=[pltpu.VMEM((units, rows), jnp.bfloat16)],
        compiler_params=pltpu.CompilerParams(vmem_limit_bytes=16 << 20),
        cost_estimate=small_cost,
        name="hidden_block",
    )(*parts, *grads, up, down, emb)


def combine_kernel(a_ref, b_ref, c_ref, d_ref, *outs):
    units = outs[0].shape[0] * 4
    width = a_ref.shape[1]
    tiles = (a_ref.shape[0] - units) // 3
    refs = (a_ref, b_ref, c_ref, d_ref)
    up = None
    for r in refs:
        term = r[0:units].astype(jnp.float32)
        up = term if up is None else up + term
    sg = jnp.concatenate([r[units : units + 2 * tiles] for r in refs], axis=0)
    low, high = units + 2 * tiles, units + 3 * tiles
    pool = jnp.concatenate(
        [r[low:high, h * units : (h + 1) * units] for r in refs for h in range(2)], axis=0
    )
    down = f32_dot(pool, sg, tn)
    sub = units // 4
    for q, out in enumerate(outs):
        out[:, 0:width] = up[q * sub : (q + 1) * sub].astype(out.dtype)
        out[:, width : 2 * width] = down[q * sub : (q + 1) * sub].astype(out.dtype)


def combine(payloads, units):
    width = payloads[0].shape[1]
    shape = lambda dtype: jax.ShapeDtypeStruct((units // 4, 2 * width), dtype)
    return pl.pallas_call(
        combine_kernel,
        out_shape=(shape(jnp.bfloat16),) * 3 + (shape(jnp.float32),),
        in_specs=[VMEM] * 4,
        out_specs=(VMEM,) * 4,
        compiler_params=pltpu.CompilerParams(vmem_limit_bytes=16 << 20),
        cost_estimate=small_cost,
        name="combine",
    )(*payloads)


def embed_kernel(table_ref, mean_ref, emb_ref, other_ref, *outs):
    tiles = mean_ref.shape[0]
    embed = (mean_ref[...] + emb_ref[0:tiles] + other_ref[...]).astype(jnp.bfloat16)
    sorted_rows = f32_dot(table_ref[...], embed, tn).astype(jnp.bfloat16)
    for k, out in enumerate(outs):
        out[...] = sorted_rows[16 * k : 16 * k + 16]


def embed_rows(table, mean, emb, other):
    width = mean.shape[1]
    return pl.pallas_call(
        embed_kernel,
        out_shape=(jax.ShapeDtypeStruct((16, width), jnp.bfloat16),) * 4,
        in_specs=[VMEM] * 4,
        out_specs=(VMEM,) * 4,
        compiler_params=pltpu.CompilerParams(vmem_limit_bytes=4 << 20),
        cost_estimate=small_cost,
        name="embed_rows",
    )(table, mean, emb, other)


def second_kernel(own_ref, *rest):
    z = lax.axis_index("enc") % 4
    received, embeds = rest[0:3], rest[3:7]
    own_out, pays, embed_out, total = rest[7], rest[8:11], rest[11], rest[12]
    width = own_out.shape[1]
    last = own_ref.shape[0] // 4
    total[...] = own_ref[...] + sum(r[...].astype(jnp.float32) for r in received)
    row = lax.broadcasted_iota(jnp.int32, (64, 64), 0)
    col = lax.broadcasted_iota(jnp.int32, (64, 64), 1)
    match = None
    for j in range(4):
        for k in range(4):
            rank = row - (16 * j + 3 * k)
            hit = (rank >= 0) & (rank < 3) & (col == 16 * k + 3 * j + rank)
            match = hit if match is None else match | hit
    embeds = jnp.concatenate([e[...] for e in embeds], axis=0)
    embeds = f32_dot(match.astype(jnp.bfloat16), embeds)
    for j in range(4):
        rows = pl.ds(pl.multiple_of(lax.rem(z + j, 4) * last, 8), last)
        up, down = total[rows, 0:width], total[rows, width : 2 * width]
        if j == 0:
            own_out[...] = jnp.concatenate([up, down], axis=0)
            embed_out[...] = embeds[0:16].astype(jnp.bfloat16)
        else:
            pays[j - 1][...] = jnp.concatenate(
                [up, down, embeds[16 * j : 16 * j + 16]], axis=0
            ).astype(jnp.bfloat16)


def second_sum(own, received, embeds):
    sub, width = own.shape[0], own.shape[1] // 2
    rows = sub // 2
    return pl.pallas_call(
        second_kernel,
        out_shape=(
            jax.ShapeDtypeStruct((rows, width), jnp.float32),
            *[jax.ShapeDtypeStruct((rows + 16, width), jnp.bfloat16)] * 3,
            jax.ShapeDtypeStruct((16, width), jnp.bfloat16),
        ),
        in_specs=[VMEM] * 8,
        out_specs=(VMEM,) * 5,
        scratch_shapes=[pltpu.VMEM(own.shape, jnp.float32)],
        compiler_params=pltpu.CompilerParams(vmem_limit_bytes=8 << 20),
        cost_estimate=small_cost,
        name="second_sum",
    )(own, *received, *embeds)


def last_kernel(place_ref, own_ref, embed_ref, a_ref, b_ref, c_ref, up_ref, down_ref, out_ref):
    half = up_ref.shape[0]
    rows = 2 * half
    total = own_ref[...]
    for r in (a_ref, b_ref, c_ref):
        total = total + r[...].astype(jnp.float32)[0:rows]
    up_ref[...] = total[0:half]
    down_ref[...] = total[half:rows]
    embeds = jnp.concatenate(
        [embed_ref[...]] + [r[rows : rows + 16] for r in (a_ref, b_ref, c_ref)], axis=0
    )
    out_ref[...] = f32_dot(place_ref[...], embeds).astype(jnp.bfloat16)


def last_sum(place, own, embed, received):
    rows, width = own.shape
    return pl.pallas_call(
        last_kernel,
        out_shape=(
            jax.ShapeDtypeStruct((rows // 2, width), jnp.float32),
            jax.ShapeDtypeStruct((rows // 2, width), jnp.float32),
            jax.ShapeDtypeStruct((place.shape[0], width), jnp.bfloat16),
        ),
        in_specs=[VMEM] * 6,
        out_specs=(VMEM,) * 3,
        compiler_params=pltpu.CompilerParams(vmem_limit_bytes=4 << 20),
        cost_estimate=small_cost,
        name="last_sum",
    )(place, own, embed, *received)


def move(value, stage, hop):
    pairs = []
    for x in range(4):
        for c in range(2):
            for y in range(4):
                for z in range(4):
                    to = [x, c, y, z]
                    if stage == 0:
                        to[1] = 1 - c
                    else:
                        spot = {1: 2 * c, 2: 2 - 2 * c, 3: 3, 4: 2}[stage]
                        to[spot] = (to[spot] + hop) % 4
                    line = lambda p: (p[0] * 2 + p[1]) * 16 + p[2] * 4 + p[3]
                    pairs.append((line((x, c, y, z)), line(to)))
    return lax.ppermute(value, axes, pairs)


def body(tile_maps, tile_owner, tissue_counts, embed_grad, depth_kernel, up_weight, down_weight):
    lane_count = lax.axis_size("enc")
    maps = jnp.transpose(tile_maps[0], (1, 2, 0, 3))
    side, _, tiles, width = maps.shape
    units = up_weight.shape[0] // 8
    capacity = embed_grad.shape[3]

    fetched = lax.all_to_all(
        jnp.transpose(embed_grad[0, 0], (1, 0, 2)), "enc", split_axis=1, concat_axis=1, tiled=True
    )

    normed, map_mean, table, send_table, place, *weights = conv_norm(
        tissue_counts, tile_owner, maps, depth_kernel, up_weight, down_weight, capacity
    )
    normed = normed.reshape(-1, width)
    sib_normed = move(normed, 0, 0)

    slot_grad = f32_dot(table, fetched.reshape(capacity * lane_count, width)).astype(jnp.bfloat16)
    sib_grad = move(slot_grad, 0, 0)

    emb = jnp.zeros((2 * tiles, width), jnp.float32)
    payloads = []
    for n, hop in enumerate(hops + (0,)):
        if not hop:
            emb, payloads[0] = lax.optimization_barrier((emb, payloads[0]))
        pay, emb = hidden_block(
            (normed, sib_normed), (slot_grad, sib_grad), weights[n], weights[4 + n], emb
        )
        payloads.append(move(pay, 1, hop) if hop else pay)

    other_emb = move(emb[tiles:], 0, 0)
    payloads[1], other_emb = lax.optimization_barrier((payloads[1], other_emb))
    rows_out = embed_rows(send_table, map_mean, emb, other_emb)
    payloads, rows_out = lax.optimization_barrier((payloads, rows_out))

    parts = combine(payloads, units)
    received = [move(parts[hop - 1], 2, hop) for hop in hops]
    by_hop = {hop: move(rows_out[hop], 4, hop) for hop in hops}
    by_hop[0] = rows_out[0]
    own, *pays, own_embed = second_sum(parts[3], received, [by_hop[hop] for hop in range(4)])
    by_hop = {hop: move(pays[hop - 1], 3, hop) for hop in hops}
    up_part, down_part, arrived = last_sum(
        place, own, own_embed, [by_hop[hop] for hop in (1, 2, 3)]
    )
    slide_embed = jnp.transpose(arrived.reshape(capacity, lane_count, width), (1, 0, 2))
    return slide_embed[None, None], up_part, down_part


def solution(mesh):
    in_specs = (
        P("slide", "enc", None, None, None),
        P("slide", "enc", None),
        P("slide", None),
        P("slide", "enc", None, None, None),
        P(),
        P(),
        P(),
    )
    out_specs = (
        P("slide", "enc", None, None, None),
        P(("slide", "enc"), None),
        P(("slide", "enc"), None),
    )
    return jax.shard_map(body, mesh=mesh, in_specs=in_specs, out_specs=out_specs, check_vma=False)
```

profile of v0, /device:TPU:0, one launch (start us, length us, event | category | flops | bytes accessed | tf_op | source)
XLA Modules:
  0.0 93.9 jit_solution(13335761416889488114)
XLA Ops:
  0.6 0.0 copy-start
  0.6 0.9 copy-done
  1.5 0.0 copy-start.1
  1.5 0.7 copy-done.1
  2.2 0.7 copy-done.2
  2.8 15.1 %conv_norm.1 = (bf16[49,32,768]{2,1,0:T(8,128)(2,1)S(1)}, f32[32,768]{1,0:T(8,128)S(1)}, bf16[32,48]{1,0:T(8,128)(2,1)S(1)}, bf16[32,64]{1,0:T(8,128)(2,1)S(1)},...) custom-call(s32[1,16]{1,0:T(1,128)S(1)} %copy-done.1, ...), custom_call_target="tpu_custom_call" | custom-call | flops 1000 | bytes 1000 | tf_op jit(solution)/shard_map/conv_norm/pallas_call | solution.py:139
  18.0 0.1 collective-permute-start
  18.1 0.0 copy-done.3
  18.1 0.1 copy.14
  18.2 15.7 %all_to_all.5 = bf16[3,16,768]{2,0,1:T(4,128)(2,1)S(1)} all-to-all(bf16[3,16,768]{2,0,1:T(4,128)(2,1)S(1)} %bitcast.25), channel_id=1, replica_groups=mesh['slide'=8,'enc'=16] {'enc'}, dimensions={1} | all-to-all | bytes 147456 | tf_op jit(solution)/shard_map/all_to_all | solution.py:428
  33.8 0.1 convolution_convert_fusion.rest_2_
  34.0 0.1 collective-permute-start.1
  34.1 1.2 %collective-permute-done.1.rest_3_ = bf16[32,768]{1,0:T(8,128)(2,1)S(1)} collective-permute-done((bf16[32,768]{1,0:T(8,128)(2,1)S(1)}, bf16[32,768]{1,0:T(8,128)(2,1)S(1)}, u32[]{:S(2)}, u32[]{:S(2)}) %collective-permute-start.1) | collective-permute-done | bytes 49184 | tf_op jit(solution)/shard_map/ppermute | solution.py:418
  35.3 0.0 collective-permute-done.rest_1_
  35.3 5.7 %hidden_block.4 = (bf16[480,768]{1,0:T(8,128)(2,1)S(1)}, f32[64,768]{1,0:T(8,128)S(1)}) custom-call(bf16[1568,768]{1,0:T(8,128)(2,1)S(1)} %bitcast.19, bf16[1568,768]{1,0:T(8,128)(2,1)S(1)} %collective-permute-done.rest_1_, bf16[32,768]{1,0:T(8,128)(2,1)S(1)} %convolution_convert_fusion.rest_2_, bf16[32,768]{1,0:T(8,128)(2,1)S(1)} %collective-permute-done.1.rest_3_, ...), custom_call_target="tpu_custom_call" | custom-call | flops 1000 | bytes 1000 | tf_op jit(solution)/shard_map/hidden_block/pallas_call | solution.py:254
  41.0 3.3 %collective-permute-start.2 = (bf16[480,768]{1,0:T(8,128)(2,1)S(1)}, bf16[480,768]{1,0:T(8,128)(2,1)S(1)}, u32[]{:S(2)}, u32[]{:S(2)}) collective-permute-start(bf16[480,768]{1,0:T(8,128)(2,1)S(1)} %get-tuple-element.64), channel_id=1, source_target_pairs={{0,64},{1,65},{2,66},{3,67},{4,68},{5,69},{6,70},{7,71},{8,72},{9,... | collective-permute-start | bytes 2211848 | tf_op jit(solution)/shard_map/ppermute | solution.py:418
  44.3 5.7 %hidden_block.5 = (bf16[480,768]{1,0:T(8,128)(2,1)S(1)}, f32[64,768]{1,0:T(8,128)S(1)}) custom-call(bf16[1568,768]{1,0:T(8,128)(2,1)S(1)} %bitcast.20, bf16[1568,768]{1,0:T(8,128)(2,1)S(1)} %collective-permute-done.rest_1_, bf16[32,768]{1,0:T(8,128)(2,1)S(1)} %convolution_convert_fusion.rest_2_, bf16[32,768]{1,0:T(8,128)(2,1)S(1)} %collective-permute-done.1.rest_3_, ...), custom_call_target="tpu_custom_call" | custom-call | flops 1000 | bytes 1000 | tf_op jit(solution)/shard_map/hidden_block/pallas_call | solution.py:254
  49.9 0.7 collective-permute-start.3
  50.6 5.7 %hidden_block.6 = (bf16[480,768]{1,0:T(8,128)(2,1)S(1)}, f32[64,768]{1,0:T(8,128)S(1)}) custom-call(bf16[1568,768]{1,0:T(8,128)(2,1)S(1)} %bitcast.21, bf16[1568,768]{1,0:T(8,128)(2,1)S(1)} %collective-permute-done.rest_1_, bf16[32,768]{1,0:T(8,128)(2,1)S(1)} %convolution_convert_fusion.rest_2_, bf16[32,768]{1,0:T(8,128)(2,1)S(1)} %collective-permute-done.1.rest_3_, ...), custom_call_target="tpu_custom_call" | custom-call | flops 1000 | bytes 1000 | tf_op jit(solution)/shard_map/hidden_block/pallas_call | solution.py:254
  56.2 2.9 %collective-permute-start.5 = (bf16[480,768]{1,0:T(8,128)(2,1)S(1)}, bf16[480,768]{1,0:T(8,128)(2,1)S(1)}, u32[]{:S(2)}, u32[]{:S(2)}) collective-permute-start(bf16[480,768]{1,0:T(8,128)(2,1)S(1)} %get-tuple-element.72), channel_id=1, source_target_pairs={{0,96},{1,97},{2,98},{3,99},{4,100},{5,101},{6,102},{7,103},{8,104... | collective-permute-start | bytes 2211848 | tf_op jit(solution)/shard_map/ppermute | solution.py:418
  59.2 0.0 collective-permute-done.2.a_ref
  59.2 5.7 %hidden_block.7 = (bf16[480,768]{1,0:T(8,128)(2,1)S(1)}, f32[64,768]{1,0:T(8,128)S(1)}) custom-call(bf16[1568,768]{1,0:T(8,128)(2,1)S(1)} %bitcast.22, bf16[1568,768]{1,0:T(8,128)(2,1)S(1)} %collective-permute-done.rest_1_, bf16[32,768]{1,0:T(8,128)(2,1)S(1)} %convolution_convert_fusion.rest_2_, bf16[32,768]{1,0:T(8,128)(2,1)S(1)} %collective-permute-done.1.rest_3_, ...), custom_call_target="tpu_custom_call" | custom-call | flops 1000 | bytes 1000 | tf_op jit(solution)/shard_map/hidden_block/pallas_call | solution.py:254
  64.8 0.1 collective-permute-start.4
  64.9 0.0 collective-permute-done.3.b_ref
  65.0 1.3 %collective-permute-done.4.other_ref = f32[32,768]{1,0:T(8,128)S(1)} collective-permute-done((f32[32,768]{1,0:T(8,128)S(1)}, f32[32,768]{1,0:T(8,128)S(1)}, u32[]{:S(2)}, u32[]{:S(2)}) %collective-permute-start.4) | collective-permute-done | bytes 98336 | tf_op jit(solution)/shard_map/ppermute | solution.py:418
  66.2 0.2 embed_rows.1
  66.4 1.7 %collective-permute-done.5.c_ref = bf16[480,768]{1,0:T(8,128)(2,1)S(1)} collective-permute-done((bf16[480,768]{1,0:T(8,128)(2,1)S(1)}, bf16[480,768]{1,0:T(8,128)(2,1)S(1)}, u32[]{:S(2)}, u32[]{:S(2)}) %collective-permute-start.5) | collective-permute-done | bytes 737312 | tf_op jit(solution)/shard_map/ppermute | solution.py:418
  68.2 0.7 combine.1
  68.8 1.3 %collective-permute-start.6 = (bf16[96,1536]{1,0:T(8,128)(2,1)S(1)}, bf16[96,1536]{1,0:T(8,128)(2,1)S(1)}, u32[]{:S(2)}, u32[]{:S(2)}) collective-permute-start(bf16[96,1536]{1,0:T(8,128)(2,1)S(1)} %get-tuple-element.86), channel_id=1, source_target_pairs={{0,8},{1,9},{2,10},{3,11},{4,12},{5,13},{6,14},{7,15},{8,0},{9,1},... | collective-permute-start | bytes 884744 | tf_op jit(solution)/shard_map/ppermute | solution.py:418
  70.1 0.7 collective-permute-start.7
  70.9 2.5 %collective-permute-start.8 = (bf16[96,1536]{1,0:T(8,128)(2,1)S(1)}, bf16[96,1536]{1,0:T(8,128)(2,1)S(1)}, u32[]{:S(2)}, u32[]{:S(2)}) collective-permute-start(bf16[96,1536]{1,0:T(8,128)(2,1)S(1)} %get-tuple-element.88), channel_id=1, source_target_pairs={{0,12},{1,13},{2,14},{3,15},{4,0},{5,1},{6,2},{7,3},{8,4},{9,5},{1... | collective-permute-start | bytes 884744 | tf_op jit(solution)/shard_map/ppermute | solution.py:418
  73.4 0.0 collective-permute-start.9
  73.4 2.2 %collective-permute-start.10 = (bf16[16,768]{1,0:T(8,128)(2,1)S(1)}, bf16[16,768]{1,0:T(8,128)(2,1)S(1)}, u32[]{:S(2)}, u32[]{:S(2)}) collective-permute-start(bf16[16,768]{1,0:T(8,128)(2,1)S(1)} %get-tuple-element.91), channel_id=1, source_target_pairs={{0,8},{1,9},{2,10},{3,11},{4,12},{5,13},{6,14},{7,15},{8,0},{9,1},... | collective-permute-start | bytes 73736 | tf_op jit(solution)/shard_map/ppermute | solution.py:418
  75.6 5.5 %collective-permute-done.9.rest_4_ = bf16[16,768]{1,0:T(8,128)(2,1)S(1)} collective-permute-done((bf16[16,768]{1,0:T(8,128)(2,1)S(1)}, bf16[16,768]{1,0:T(8,128)(2,1)S(1)}, u32[]{:S(2)}, u32[]{:S(2)}) %collective-permute-start.9) | collective-permute-done | bytes 24608 | tf_op jit(solution)/shard_map/ppermute | solution.py:418
  81.1 0.6 collective-permute-start.11
  81.7 0.0 collective-permute-done.10.rest_5_
  81.7 3.2 %collective-permute-done.11.rest_6_ = bf16[16,768]{1,0:T(8,128)(2,1)S(1)} collective-permute-done((bf16[16,768]{1,0:T(8,128)(2,1)S(1)}, bf16[16,768]{1,0:T(8,128)(2,1)S(1)}, u32[]{:S(2)}, u32[]{:S(2)}) %collective-permute-start.11) | collective-permute-done | bytes 24608 | tf_op jit(solution)/shard_map/ppermute | solution.py:418
  84.9 0.0 collective-permute-done.6.rest_0_
  84.9 0.0 collective-permute-done.7.rest_1_
  84.9 0.0 collective-permute-done.8.rest_2_
  84.9 0.4 second_sum.1
  85.3 0.6 collective-permute-start.12
  85.9 2.2 %collective-permute-start.13 = (bf16[64,768]{1,0:T(8,128)(2,1)S(1)}, bf16[64,768]{1,0:T(8,128)(2,1)S(1)}, u32[]{:S(2)}, u32[]{:S(2)}) collective-permute-start(bf16[64,768]{1,0:T(8,128)(2,1)S(1)} %get-tuple-element.96), channel_id=1, source_target_pairs={{0,2},{1,3},{2,0},{3,1},{4,6},{5,7},{6,4},{7,5},{8,10},{9,11},{10,... | collective-permute-start | bytes 294920 | tf_op jit(solution)/shard_map/ppermute | solution.py:418
  88.1 1.4 %collective-permute-start.14 = (bf16[64,768]{1,0:T(8,128)(2,1)S(1)}, bf16[64,768]{1,0:T(8,128)(2,1)S(1)}, u32[]{:S(2)}, u32[]{:S(2)}) collective-permute-start(bf16[64,768]{1,0:T(8,128)(2,1)S(1)} %get-tuple-element.97), channel_id=1, source_target_pairs={{0,3},{1,0},{2,1},{3,2},{4,7},{5,4},{6,5},{7,6},{8,11},{9,8},{10,9... | collective-permute-start | bytes 294920 | tf_op jit(solution)/shard_map/ppermute | solution.py:418
  89.5 2.8 %collective-permute-done.12.a_ref = bf16[64,768]{1,0:T(8,128)(2,1)S(1)} collective-permute-done((bf16[64,768]{1,0:T(8,128)(2,1)S(1)}, bf16[64,768]{1,0:T(8,128)(2,1)S(1)}, u32[]{:S(2)}, u32[]{:S(2)}) %collective-permute-start.12) | collective-permute-done | bytes 98336 | tf_op jit(solution)/shard_map/ppermute | solution.py:418
  92.2 0.0 collective-permute-done.13.b_ref
  92.2 0.9 collective-permute-done.14.c_ref
  93.1 0.8 last_sum.1
  (5 shorter events, 0.0 us)
Async XLA Ops:
  0.6 0.9 copy-start
  1.5 0.7 copy-start.1
  2.2 0.7 copy-start.2
  2.8 15.2 %copy-start.3 = (bf16[1,1,16,3,768]{4,2,3,1,0:T(8,128)(2,1)S(1)}, bf16[1,1,16,3,768]{4,2,3,1,0:T(8,128)(2,1)}, u32[]{:S(2)}) copy-start(bf16[1,1,16,3,768]{4,2,3,1,0:T(8,128)(2,1)} %param.10) | copy-start | bytes 221188
  18.0 17.3 %collective-permute-start = (bf16[1568,768]{1,0:T(8,128)(2,1)S(1)}, bf16[1568,768]{1,0:T(8,128)(2,1)S(1)}, u32[]{:S(2)}, u32[]{:S(2)}) collective-permute-start(bf16[1568,768]{1,0:T(8,128)(2,1)S(1)} %bitcast.18), channel_id=1, source_target_pairs={{0,16},{1,17},{2,18},{3,19},{4,20},{5,21},{6,22},{7,23},{8,24},{9,... | collective-permute-start | bytes 7225352 | tf_op jit(solution)/shard_map/ppermute | solution.py:418
  34.0 1.3 %collective-permute-start.1 = (bf16[32,768]{1,0:T(8,128)(2,1)S(1)}, bf16[32,768]{1,0:T(8,128)(2,1)S(1)}, u32[]{:S(2)}, u32[]{:S(2)}) collective-permute-start(bf16[32,768]{1,0:T(8,128)(2,1)S(1)} %convolution_convert_fusion.rest_2_), channel_id=1, source_target_pairs={{0,16},{1,17},{2,18},{3,19},{4,20},{5,21},{6,22},{7,23},{8,24},{9,... | collective-permute-start | bytes 147464 | tf_op jit(solution)/shard_map/ppermute | solution.py:418
  41.0 18.2 %collective-permute-start.2 = (bf16[480,768]{1,0:T(8,128)(2,1)S(1)}, bf16[480,768]{1,0:T(8,128)(2,1)S(1)}, u32[]{:S(2)}, u32[]{:S(2)}) collective-permute-start(bf16[480,768]{1,0:T(8,128)(2,1)S(1)} %get-tuple-element.64), channel_id=1, source_target_pairs={{0,64},{1,65},{2,66},{3,67},{4,68},{5,69},{6,70},{7,71},{8,72},{9,... | collective-permute-start | bytes 2211848 | tf_op jit(solution)/shard_map/ppermute | solution.py:418
  49.9 15.0 %collective-permute-start.3 = (bf16[480,768]{1,0:T(8,128)(2,1)S(1)}, bf16[480,768]{1,0:T(8,128)(2,1)S(1)}, u32[]{:S(2)}, u32[]{:S(2)}) collective-permute-start(bf16[480,768]{1,0:T(8,128)(2,1)S(1)} %get-tuple-element.66), channel_id=1, source_target_pairs={{0,32},{1,33},{2,34},{3,35},{4,36},{5,37},{6,38},{7,39},{8,40},{9,... | collective-permute-start | bytes 2211848 | tf_op jit(solution)/shard_map/ppermute | solution.py:418
  56.2 11.9 %collective-permute-start.5 = (bf16[480,768]{1,0:T(8,128)(2,1)S(1)}, bf16[480,768]{1,0:T(8,128)(2,1)S(1)}, u32[]{:S(2)}, u32[]{:S(2)}) collective-permute-start(bf16[480,768]{1,0:T(8,128)(2,1)S(1)} %get-tuple-element.72), channel_id=1, source_target_pairs={{0,96},{1,97},{2,98},{3,99},{4,100},{5,101},{6,102},{7,103},{8,104... | collective-permute-start | bytes 2211848 | tf_op jit(solution)/shard_map/ppermute | solution.py:418
  64.8 1.4 %collective-permute-start.4 = (f32[32,768]{1,0:T(8,128)S(1)}, f32[32,768]{1,0:T(8,128)S(1)}, u32[]{:S(2)}, u32[]{:S(2)}) collective-permute-start(f32[32,768]{1,0:T(8,128)S(1)} %slice.3), channel_id=1, source_target_pairs={{0,16},{1,17},{2,18},{3,19},{4,20},{5,21},{6,22},{7,23},{8,24},{9,... | collective-permute-start | bytes 294920 | tf_op jit(solution)/shard_map/ppermute | solution.py:418
  68.8 16.1 %collective-permute-start.6 = (bf16[96,1536]{1,0:T(8,128)(2,1)S(1)}, bf16[96,1536]{1,0:T(8,128)(2,1)S(1)}, u32[]{:S(2)}, u32[]{:S(2)}) collective-permute-start(bf16[96,1536]{1,0:T(8,128)(2,1)S(1)} %get-tuple-element.86), channel_id=1, source_target_pairs={{0,8},{1,9},{2,10},{3,11},{4,12},{5,13},{6,14},{7,15},{8,0},{9,1},... | collective-permute-start | bytes 884744 | tf_op jit(solution)/shard_map/ppermute | solution.py:418
  70.1 14.8 %collective-permute-start.7 = (bf16[96,1536]{1,0:T(8,128)(2,1)S(1)}, bf16[96,1536]{1,0:T(8,128)(2,1)S(1)}, u32[]{:S(2)}, u32[]{:S(2)}) collective-permute-start(bf16[96,1536]{1,0:T(8,128)(2,1)S(1)} %get-tuple-element.87), channel_id=1, source_target_pairs={{0,4},{1,5},{2,6},{3,7},{4,8},{5,9},{6,10},{7,11},{8,12},{9,13},{1... | collective-permute-start | bytes 884744 | tf_op jit(solution)/shard_map/ppermute | solution.py:418
  70.9 14.1 %collective-permute-start.8 = (bf16[96,1536]{1,0:T(8,128)(2,1)S(1)}, bf16[96,1536]{1,0:T(8,128)(2,1)S(1)}, u32[]{:S(2)}, u32[]{:S(2)}) collective-permute-start(bf16[96,1536]{1,0:T(8,128)(2,1)S(1)} %get-tuple-element.88), channel_id=1, source_target_pairs={{0,12},{1,13},{2,14},{3,15},{4,0},{5,1},{6,2},{7,3},{8,4},{9,5},{1... | collective-permute-start | bytes 884744 | tf_op jit(solution)/shard_map/ppermute | solution.py:418
  73.4 7.7 %collective-permute-start.9 = (bf16[16,768]{1,0:T(8,128)(2,1)S(1)}, bf16[16,768]{1,0:T(8,128)(2,1)S(1)}, u32[]{:S(2)}, u32[]{:S(2)}) collective-permute-start(bf16[16,768]{1,0:T(8,128)(2,1)S(1)} %get-tuple-element.90), channel_id=1, source_target_pairs={{0,4},{1,5},{2,6},{3,7},{4,8},{5,9},{6,10},{7,11},{8,12},{9,13},{1... | collective-permute-start | bytes 73736 | tf_op jit(solution)/shard_map/ppermute | solution.py:418
  73.4 8.3 %collective-permute-start.10 = (bf16[16,768]{1,0:T(8,128)(2,1)S(1)}, bf16[16,768]{1,0:T(8,128)(2,1)S(1)}, u32[]{:S(2)}, u32[]{:S(2)}) collective-permute-start(bf16[16,768]{1,0:T(8,128)(2,1)S(1)} %get-tuple-element.91), channel_id=1, source_target_pairs={{0,8},{1,9},{2,10},{3,11},{4,12},{5,13},{6,14},{7,15},{8,0},{9,1},... | collective-permute-start | bytes 73736 | tf_op jit(solution)/shard_map/ppermute | solution.py:418
  81.1 3.8 %collective-permute-start.11 = (bf16[16,768]{1,0:T(8,128)(2,1)S(1)}, bf16[16,768]{1,0:T(8,128)(2,1)S(1)}, u32[]{:S(2)}, u32[]{:S(2)}) collective-permute-start(bf16[16,768]{1,0:T(8,128)(2,1)S(1)} %get-tuple-element.92), channel_id=1, source_target_pairs={{0,12},{1,13},{2,14},{3,15},{4,0},{5,1},{6,2},{7,3},{8,4},{9,5},{1... | collective-permute-start | bytes 73736 | tf_op jit(solution)/shard_map/ppermute | solution.py:418
  85.3 7.0 %collective-permute-start.12 = (bf16[64,768]{1,0:T(8,128)(2,1)S(1)}, bf16[64,768]{1,0:T(8,128)(2,1)S(1)}, u32[]{:S(2)}, u32[]{:S(2)}) collective-permute-start(bf16[64,768]{1,0:T(8,128)(2,1)S(1)} %get-tuple-element.95), channel_id=1, source_target_pairs={{0,1},{1,2},{2,3},{3,0},{4,5},{5,6},{6,7},{7,4},{8,9},{9,10},{10,1... | collective-permute-start | bytes 294920 | tf_op jit(solution)/shard_map/ppermute | solution.py:418
  85.9 6.4 %collective-permute-start.13 = (bf16[64,768]{1,0:T(8,128)(2,1)S(1)}, bf16[64,768]{1,0:T(8,128)(2,1)S(1)}, u32[]{:S(2)}, u32[]{:S(2)}) collective-permute-start(bf16[64,768]{1,0:T(8,128)(2,1)S(1)} %get-tuple-element.96), channel_id=1, source_target_pairs={{0,2},{1,3},{2,0},{3,1},{4,6},{5,7},{6,4},{7,5},{8,10},{9,11},{10,... | collective-permute-start | bytes 294920 | tf_op jit(solution)/shard_map/ppermute | solution.py:418
  88.1 5.0 %collective-permute-start.14 = (bf16[64,768]{1,0:T(8,128)(2,1)S(1)}, bf16[64,768]{1,0:T(8,128)(2,1)S(1)}, u32[]{:S(2)}, u32[]{:S(2)}) collective-permute-start(bf16[64,768]{1,0:T(8,128)(2,1)S(1)} %get-tuple-element.97), channel_id=1, source_target_pairs={{0,3},{1,0},{2,1},{3,2},{4,7},{5,4},{6,5},{7,6},{8,11},{9,8},{10,9... | collective-permute-start | bytes 294920 | tf_op jit(solution)/shard_map/ppermute | solution.py:418
where the time goes:
time: 94.4 us; the launch traced here: 93.9 us
  Pallas kernels  39.8 us (42%)
  starting transfers between devices  18.6 us (20%)
  waiting for transfers between devices  16.6 us (18%)
  blocking collectives  15.7 us (17%)
  local copies, waits for them, and re-layouts  2.28 us (2%)
    pallas_call x4, Pallas kernels, hidden_block(): pl.pallas_call(block_kernel, out_shape=(jax.ShapeDtypeStruct((units + 3 *...  22.6 us
    ppermute x15, starting transfers between devices, move(): return lax.ppermute(value, axes, pairs)  18.6 us
    ppermute x15, waiting for transfers between devices, move(): return lax.ppermute(value, axes, pairs)  16.6 us
    all_to_all x1, blocking collectives, body(): lax.all_to_all(jnp.transpose(embed_grad[0, 0], (1, 0, 2)), 'enc', split_a...  15.7 us
    pallas_call x1, Pallas kernels, conv_norm(): pl.pallas_call(conv_kernel, out_shape=(shape((cells, tiles, width), jnp.b...  15.1 us
    unnamed x9, local copies, waits for them, and re-layouts  2.25 us
  transfers between devices with their start and end apart: 15, of which 7 were waited for; matrix products, arithmetic and copies ran while one was open for 0% of the time, Pallas kernels for 18%

commit v1 on v0

--- a/solution.py
+++ b/solution.py
@@ -16,6 +16,7 @@
 SMEM = pl.BlockSpec(memory_space=pltpu.SMEM)
 HBM = pl.BlockSpec(memory_space=pltpu.HBM)
 small_cost = pl.CostEstimate(flops=1000, bytes_accessed=1000, transcendentals=0)
+large_cost = pl.CostEstimate(flops=20_000_000_000, bytes_accessed=1000, transcendentals=0)
 nt = (((1,), (1,)), ((), ()))
 tn = (((0,), (0,)), ((), ()))
 
@@ -29,7 +30,7 @@
 
 
 def slot_tables(counts_ref, owners_ref, table_ref, send_ref, place_ref):
-    enc = lax.axis_index("enc")
+    enc, core = lax.axis_index("enc"), lax.axis_index("slide") % 2
     count, y, z = counts_ref[0, enc], enc // 4, enc % 4
     lanes, tiles = counts_ref.shape[1], owners_ref.shape[1]
     slot = lax.broadcasted_iota(jnp.int32, (tiles, tiles), 0)
@@ -41,13 +42,17 @@
     rank = jnp.sum(same, axis=1, keepdims=True).astype(jnp.int32)
     live = lax.broadcasted_iota(jnp.int32, (tiles, 1), 0) < count
     pick = lambda index, size, on: jnp.where(row_hits(index, size) & on, 1.0, 0.0).astype(jnp.bfloat16)
-    table_ref[...] = pick(rank * lanes + owners, table_ref.shape[1], live)
     hops_y, hops_z = ((owners >> 2) - y) & 3, ((owners & 3) - z) & 3
-    send_ref[...] = pick(hops_y * 16 + hops_z * 3 + rank, send_ref.shape[1], live)
+    table_ref[...] = pick(((4 - hops_z) & 3) * 16 + ((4 - hops_y) & 3) * 3 + rank, 64, live)
+    one, two = (hops_z, hops_y), (hops_y, hops_z)
+    near, far = [jnp.where(core == 0, p, q) for p, q in zip(one, two)]
+    send_ref[...] = pick(near * 16 + far * 3 + rank, 64, live)
     spots = lax.broadcasted_iota(jnp.int32, (place_ref.shape[0], 1), 0)
     reader = spots & (lanes - 1)
     from_y, from_z = (y - (reader >> 2)) & 3, (z - (reader & 3)) & 3
-    place_ref[...] = pick(from_z * 16 + from_y * 3 + (spots >> 4), place_ref.shape[1], spots >= 0)
+    near = jnp.where(core == 0, from_z, from_y)
+    far = jnp.where(core == 0, from_y, from_z)
+    place_ref[...] = pick(far * 16 + near * 3 + (spots >> 4), 64, spots >= 0)
 
 
 def conv_kernel(counts_ref, owners_ref, x_hbm, k_hbm, up_hbm, down_hbm, *rest):
@@ -62,7 +67,6 @@
     slide, enc = lax.axis_index("slide"), lax.axis_index("enc")
     x, core, y = slide // 2, slide % 2, enc // 4
     first = jnp.where(core == 0, x, y)
-    second = jnp.where(core == 0, y, x)
 
     def maps_copy(group):
         rows = pl.ds(group * 16, 16)
@@ -70,8 +74,7 @@
 
     def weight_copy(n):
         goal = lax.rem(first + (hops + (0,))[n % 16 // 4], 4)
-        inner = lax.rem(second + n % 4 + 1, 4)
-        row = jnp.where(core == 0, 8 * goal + inner, 8 * inner + goal) + 4 * core
+        row = jnp.where(core == 0, 8 * goal + n % 4, 8 * (n % 4) + goal) + 4 * core
         start = pl.ds(pl.multiple_of(row * sub, sub), sub)
         source = (up_hbm if n < 16 else down_hbm).at[start, :]
         goal = weights[n // 4].at[pl.ds(n % 4 * sub, sub), :]
@@ -81,9 +84,9 @@
     kernel_copy.start()
     for group in range(tiles // 16):
         maps_copy(group).start()
+    slot_tables(counts_ref, owners_ref, table_ref, send_ref, place_ref)
     for n in range(32):
         weight_copy(n).start()
-    slot_tables(counts_ref, owners_ref, table_ref, send_ref, place_ref)
     kernel_copy.wait()
     for n in range(cells):
         kf[n] = jnp.broadcast_to(
@@ -141,7 +144,7 @@
         out_shape=(
             shape((cells, tiles, width), jnp.bfloat16),
             shape((tiles, width), jnp.float32),
-            shape((tiles, 16 * capacity), jnp.bfloat16),
+            shape((tiles, 64), jnp.bfloat16),
             shape((tiles, 64), jnp.bfloat16),
             shape((16 * capacity, 64), jnp.bfloat16),
             *[shape((units, width), jnp.bfloat16)] * 8,
@@ -266,11 +269,76 @@
     )(*parts, *grads, up, down, emb)
 
 
-def combine_kernel(a_ref, b_ref, c_ref, d_ref, *outs):
-    units = outs[0].shape[0] * 4
+def one_hot_rows(target, rows):
+    hit = lax.broadcasted_iota(jnp.int32, (rows, target.shape[1]), 0) == target
+    return jnp.where(hit, 1.0, 0.0).astype(jnp.bfloat16)
+
+
+def regroup(blocks):
+    col = lax.broadcasted_iota(jnp.int32, (1, 64), 1)
+    spot = col & 15
+    far = jnp.where(spot < 3, 0, jnp.where(spot < 6, 1, jnp.where(spot < 9, 2, 3)))
+    target = jnp.where(spot < 12, 16 * far + 3 * (col >> 4) + spot - 3 * far, -1)
+    return f32_dot(one_hot_rows(target, 64), jnp.concatenate(blocks, axis=0))
+
+
+def spread_kernel(grad_ref, *outs):
+    enc = lax.axis_index("enc")
+    y, z = enc // 4, enc % 4
+    col = lax.broadcasted_iota(jnp.int32, (1, grad_ref.shape[0]), 1)
+    reader = col & 15
+    target = (((reader >> 2) - y) & 3) * 16 + (((reader & 3) - z) & 3) * 3 + (col >> 4)
+    rows = f32_dot(one_hot_rows(target, 64), grad_ref[...]).astype(jnp.bfloat16)
+    for k, out in enumerate(outs):
+        out[...] = rows[16 * k : 16 * k + 16]
+
+
+def regroup_kernel(*refs):
+    rows = regroup([r[...] for r in refs[0:4]]).astype(jnp.bfloat16)
+    for k, out in enumerate(refs[4:]):
+        out[...] = rows[16 * k : 16 * k + 16]
+
+
+def slot_kernel(table_ref, *refs):
+    rows = jnp.concatenate([r[...] for r in refs[0:4]], axis=0)
+    refs[4][...] = f32_dot(table_ref[...], rows).astype(jnp.bfloat16)
+
+
+def small_call(kernel, name, args, shapes, cost):
+    return pl.pallas_call(
+        kernel,
+        out_shape=tuple(jax.ShapeDtypeStruct(dims, jnp.bfloat16) for dims in shapes),
+        in_specs=[VMEM] * len(args),
+        out_specs=(VMEM,) * len(shapes),
+        compiler_params=pltpu.CompilerParams(vmem_limit_bytes=4 << 20),
+        cost_estimate=cost,
+        name=name,
+    )(*args)
+
+
+def spread_rows(grads):
+    return small_call(spread_kernel, "spread_rows", (grads,), [(16, grads.shape[1])] * 4, small_cost)
+
+
+def regroup_rows(blocks):
+    return small_call(regroup_kernel, "regroup_rows", blocks, [blocks[0].shape] * 4, large_cost)
+
+
+def slot_rows(table, blocks):
+    dims = (table.shape[0], blocks[0].shape[1])
+    return small_call(slot_kernel, "slot_rows", (table, *blocks), [dims], large_cost)[0]
+
+
+def combine_kernel(a_ref, b_ref, c_ref, d_ref, table_ref, mean_ref, emb_ref, other_ref, *outs):
+    pays, own_out, embeds, total = outs[0:3], outs[3], outs[4:8], outs[8]
+    slide, enc = lax.axis_index("slide"), lax.axis_index("enc")
+    x, core, z = slide // 2, slide % 2, enc % 4
+    units = total.shape[0]
     width = a_ref.shape[1]
     tiles = (a_ref.shape[0] - units) // 3
     refs = (a_ref, b_ref, c_ref, d_ref)
+    embed = (mean_ref[...] + emb_ref[0:tiles] + other_ref[...]).astype(jnp.bfloat16)
+    rows = f32_dot(table_ref[...], embed, tn)
     up = None
     for r in refs:
         term = r[0:units].astype(jnp.float32)
@@ -280,78 +348,73 @@
     pool = jnp.concatenate(
         [r[low:high, h * units : (h + 1) * units] for r in refs for h in range(2)], axis=0
     )
-    down = f32_dot(pool, sg, tn)
-    sub = units // 4
-    for q, out in enumerate(outs):
-        out[:, 0:width] = up[q * sub : (q + 1) * sub].astype(out.dtype)
-        out[:, width : 2 * width] = down[q * sub : (q + 1) * sub].astype(out.dtype)
-
-
-def combine(payloads, units):
+    total[:, 0:width] = up
+    total[:, width : 2 * width] = f32_dot(pool, sg, tn)
+    sub, last = units // 4, units // 16
+    for hop in range(4):
+        pieces = []
+        for i in range(4):
+            on_z = i * sub + ((z + hop) & 3) * last
+            on_x = ((x + hop) & 3) * sub + i * last
+            start = pl.multiple_of(jnp.where(core == 0, on_z, on_x), 8)
+            pieces.append(total[pl.ds(start, last), :])
+        mine = rows[16 * hop : 16 * hop + 16]
+        embeds[hop][...] = mine.astype(jnp.bfloat16)
+        if hop:
+            pieces.append(jnp.concatenate([mine[0:8], mine[8:16]], axis=1))
+            pays[hop - 1][...] = jnp.concatenate(pieces, axis=0).astype(jnp.bfloat16)
+        else:
+            own_out[...] = jnp.concatenate(pieces, axis=0)
+
+
+def combine(payloads, units, table, mean, emb, other):
     width = payloads[0].shape[1]
-    shape = lambda dtype: jax.ShapeDtypeStruct((units // 4, 2 * width), dtype)
+    shape = jax.ShapeDtypeStruct
     return pl.pallas_call(
         combine_kernel,
-        out_shape=(shape(jnp.bfloat16),) * 3 + (shape(jnp.float32),),
-        in_specs=[VMEM] * 4,
-        out_specs=(VMEM,) * 4,
+        out_shape=(
+            *[shape((units // 4 + 8, 2 * width), jnp.bfloat16)] * 3,
+            shape((units // 4, 2 * width), jnp.float32),
+            *[shape((16, width), jnp.bfloat16)] * 4,
+        ),
+        in_specs=[VMEM] * 8,
+        out_specs=(VMEM,) * 8,
+        scratch_shapes=[pltpu.VMEM((units, 2 * width), jnp.float32)],
         compiler_params=pltpu.CompilerParams(vmem_limit_bytes=16 << 20),
         cost_estimate=small_cost,
         name="combine",
-    )(*payloads)
-
-
-def embed_kernel(table_ref, mean_ref, emb_ref, other_ref, *outs):
-    tiles = mean_ref.shape[0]
-    embed = (mean_ref[...] + emb_ref[0:tiles] + other_ref[...]).astype(jnp.bfloat16)
-    sorted_rows = f32_dot(table_ref[...], embed, tn).astype(jnp.bfloat16)
-    for k, out in enumerate(outs):
-        out[...] = sorted_rows[16 * k : 16 * k + 16]
-
-
-def embed_rows(table, mean, emb, other):
-    width = mean.shape[1]
-    return pl.pallas_call(
-        embed_kernel,
-        out_shape=(jax.ShapeDtypeStruct((16, width), jnp.bfloat16),) * 4,
-        in_specs=[VMEM] * 4,
-        out_specs=(VMEM,) * 4,
-        compiler_params=pltpu.CompilerParams(vmem_limit_bytes=4 << 20),
-        cost_estimate=small_cost,
-        name="embed_rows",
-    )(table, mean, emb, other)
+    )(*payloads, table, mean, emb, other)
 
 
 def second_kernel(own_ref, *rest):
-    z = lax.axis_index("enc") % 4
-    received, embeds = rest[0:3], rest[3:7]
+    received, own_embed, moved = rest[0:3], rest[3], rest[4:7]
     own_out, pays, embed_out, total = rest[7], rest[8:11], rest[11], rest[12]
+    core, enc = lax.axis_index("slide") % 2, lax.axis_index("enc")
+    third = jnp.where(core == 0, enc // 4, enc % 4)
     width = own_out.shape[1]
-    last = own_ref.shape[0] // 4
-    total[...] = own_ref[...] + sum(r[...].astype(jnp.float32) for r in received)
-    row = lax.broadcasted_iota(jnp.int32, (64, 64), 0)
-    col = lax.broadcasted_iota(jnp.int32, (64, 64), 1)
-    match = None
-    for j in range(4):
-        for k in range(4):
-            rank = row - (16 * j + 3 * k)
-            hit = (rank >= 0) & (rank < 3) & (col == 16 * k + 3 * j + rank)
-            match = hit if match is None else match | hit
-    embeds = jnp.concatenate([e[...] for e in embeds], axis=0)
-    embeds = f32_dot(match.astype(jnp.bfloat16), embeds)
-    for j in range(4):
-        rows = pl.ds(pl.multiple_of(lax.rem(z + j, 4) * last, 8), last)
+    sub = own_ref.shape[0]
+    last = sub // 4
+    received = [r[...].astype(jnp.float32) for r in received]
+    total[...] = own_ref[...] + sum(r[0:sub] for r in received)
+    blocks = [own_embed[...]]
+    for r, other in zip(received, moved):
+        ridden = jnp.concatenate([r[sub:, 0:width], r[sub:, width : 2 * width]], axis=0)
+        block = jnp.where(core == 0, ridden, other[...].astype(jnp.float32))
+        blocks.append(block.astype(jnp.bfloat16))
+    embeds = regroup(blocks)
+    for hop in range(4):
+        rows = pl.ds(pl.multiple_of(((third + hop) & 3) * last, 8), last)
         up, down = total[rows, 0:width], total[rows, width : 2 * width]
-        if j == 0:
+        if hop == 0:
             own_out[...] = jnp.concatenate([up, down], axis=0)
             embed_out[...] = embeds[0:16].astype(jnp.bfloat16)
         else:
-            pays[j - 1][...] = jnp.concatenate(
-                [up, down, embeds[16 * j : 16 * j + 16]], axis=0
+            pays[hop - 1][...] = jnp.concatenate(
+                [up, down, embeds[16 * hop : 16 * hop + 16]], axis=0
             ).astype(jnp.bfloat16)
 
 
-def second_sum(own, received, embeds):
+def second_sum(own, received, own_embed, moved):
     sub, width = own.shape[0], own.shape[1] // 2
     rows = sub // 2
     return pl.pallas_call(
@@ -367,7 +430,7 @@
         compiler_params=pltpu.CompilerParams(vmem_limit_bytes=8 << 20),
         cost_estimate=small_cost,
         name="second_sum",
-    )(own, *received, *embeds)
+    )(own, *received, own_embed, *moved)
 
 
 def last_kernel(place_ref, own_ref, embed_ref, a_ref, b_ref, c_ref, up_ref, down_ref, out_ref):
@@ -402,19 +465,19 @@
 
 
 def move(value, stage, hop):
+    spots = {0: (1, 1), 1: (0, 2), 2: (3, 0), 3: (2, 3), 4: (2, 2), 5: (3, 3)}[stage]
     pairs = []
     for x in range(4):
-        for c in range(2):
+        for core in range(2):
             for y in range(4):
                 for z in range(4):
-                    to = [x, c, y, z]
+                    here, there = [x, core, y, z], [x, core, y, z]
                     if stage == 0:
-                        to[1] = 1 - c
+                        there[1] = 1 - core
                     else:
-                        spot = {1: 2 * c, 2: 2 - 2 * c, 3: 3, 4: 2}[stage]
-                        to[spot] = (to[spot] + hop) % 4
+                        there[spots[core]] = (there[spots[core]] + hop) % 4
                     line = lambda p: (p[0] * 2 + p[1]) * 16 + p[2] * 4 + p[3]
-                    pairs.append((line((x, c, y, z)), line(to)))
+                    pairs.append((line(here), line(there)))
     return lax.ppermute(value, axes, pairs)
 
 
@@ -425,17 +488,18 @@
     units = up_weight.shape[0] // 8
     capacity = embed_grad.shape[3]
 
-    fetched = lax.all_to_all(
-        jnp.transpose(embed_grad[0, 0], (1, 0, 2)), "enc", split_axis=1, concat_axis=1, tiled=True
-    )
-
+    sent = spread_rows(jnp.transpose(embed_grad[0, 0], (1, 0, 2)).reshape(-1, width))
+    arrived = [move(sent[hop], 4, hop) for hop in (1, 2, 3)]
+    tissue_counts, sent = lax.optimization_barrier((tissue_counts, sent))
     normed, map_mean, table, send_table, place, *weights = conv_norm(
         tissue_counts, tile_owner, maps, depth_kernel, up_weight, down_weight, capacity
     )
     normed = normed.reshape(-1, width)
     sib_normed = move(normed, 0, 0)
-
-    slot_grad = f32_dot(table, fetched.reshape(capacity * lane_count, width)).astype(jnp.bfloat16)
+    table, arrived = lax.optimization_barrier((table, arrived))
+    sent = regroup_rows((sent[0], *arrived))
+    arrived = [move(sent[hop], 5, hop) for hop in (1, 2, 3)]
+    slot_grad = slot_rows(table, (sent[0], *arrived))
     sib_grad = move(slot_grad, 0, 0)
 
     emb = jnp.zeros((2 * tiles, width), jnp.float32)
@@ -450,15 +514,13 @@
 
     other_emb = move(emb[tiles:], 0, 0)
     payloads[1], other_emb = lax.optimization_barrier((payloads[1], other_emb))
-    rows_out = embed_rows(send_table, map_mean, emb, other_emb)
-    payloads, rows_out = lax.optimization_barrier((payloads, rows_out))
-
-    parts = combine(payloads, units)
-    received = [move(parts[hop - 1], 2, hop) for hop in hops]
-    by_hop = {hop: move(rows_out[hop], 4, hop) for hop in hops}
-    by_hop[0] = rows_out[0]
-    own, *pays, own_embed = second_sum(parts[3], received, [by_hop[hop] for hop in range(4)])
-    by_hop = {hop: move(pays[hop - 1], 3, hop) for hop in hops}
+    *pays, own, own_embed, embed_1, embed_2, embed_3 = combine(
+        payloads, units, send_table, map_mean, emb, other_emb
+    )
+    received = [move(pays[hop - 1], 2, hop) for hop in (1, 2, 3)]
+    moved = [move(rows, 4, hop) for hop, rows in ((1, embed_1), (2, embed_2), (3, embed_3))]
+    own, *pays, own_embed = second_sum(own, received, own_embed, moved)
+    by_hop = {hop: move(pays[hop - 1], 3, hop) for hop in (1, 2, 3)}
     up_part, down_part, arrived = last_sum(
         place, own, own_embed, [by_hop[hop] for hop in (1, 2, 3)]
     )

time: 94.4 us -> 92.9 us (0.984)
  blocking collectives: 15.7 us -> 0 us
  starting transfers between devices: 18.6 us -> 28.7 us
  waiting for transfers between devices: 16.6 us -> 19.2 us
    all_to_all x1 -> x0, blocking collectives: 15.7 us -> none  [body(): lax.all_to_all(jnp.transpose(embed_grad[0, 0], (1, 0, 2)), 'enc', split_a...]
    ppermute x15 -> x21, starting transfers between devices: 18.6 us -> 28.7 us  [move(): return lax.ppermute(value, axes, pairs)]
    ppermute x15 -> x21, waiting for transfers between devices: 16.6 us -> 19.2 us  [move(): return lax.ppermute(value, axes, pairs)]
    unnamed x9 -> x8, local copies, waits for them, and re-layouts: 2.25 us -> 3.07 us
  transfers between devices with their start and end apart: 15 -> 21, of which waited for: 7 -> 10; matrix products, arithmetic and copies ran while one was open for 0% -> 0% of each run, Pallas kernels for 18% -> 35%
where the time goes in v1:
time: 92.9 us; the launch traced here: 91.9 us
  Pallas kernels  40.1 us (43%)
  starting transfers between devices  28.7 us (31%)
  waiting for transfers between devices  19.2 us (21%)
  local copies, waits for them, and re-layouts  3.1 us (3%)
    ppermute x21, starting transfers between devices, move(): return lax.ppermute(value, axes, pairs)  28.7 us
    pallas_call x4, Pallas kernels, hidden_block(): pl.pallas_call(block_kernel, out_shape=(jax.ShapeDtypeStruct((units + 3 *...  22.6 us
    ppermute x21, waiting for transfers between devices, move(): return lax.ppermute(value, axes, pairs)  19.2 us
    pallas_call x1, Pallas kernels, conv_norm(): pl.pallas_call(conv_kernel, out_shape=(shape((cells, tiles, width), jnp.b...  15.1 us
    unnamed x8, local copies, waits for them, and re-layouts  3.07 us
  transfers between devices with their start and end apart: 21, of which 10 were waited for; matrix products, arithmetic and copies ran while one was open for 0% of the time, Pallas kernels for 35%

profile of v1, /device:TPU:0, one launch (start us, length us, event | category | flops | bytes accessed | tf_op | source)
XLA Modules:
  0.0 91.9 jit_solution(6554355838234673208)
XLA Ops:
  0.6 0.9 copy-done.1
  1.5 0.1 spread_rows.1
  1.7 1.7 %collective-permute-start.1 = (bf16[16,768]{1,0:T(8,128)(2,1)S(1)}, bf16[16,768]{1,0:T(8,128)(2,1)S(1)}, u32[]{:S(2)}, u32[]{:S(2)}) collective-permute-start(bf16[16,768]{1,0:T(8,128)(2,1)S(1)} %get-tuple-element.59), channel_id=1, source_target_pairs={{0,4},{1,5},{2,6},{3,7},{4,8},{5,9},{6,10},{7,11},{8,12},{9,13},{1... | collective-permute-start | bytes 73736 | tf_op jit(solution)/shard_map/ppermute | solution.py:481
  3.4 2.9 %collective-permute-start.2 = (bf16[16,768]{1,0:T(8,128)(2,1)S(1)}, bf16[16,768]{1,0:T(8,128)(2,1)S(1)}, u32[]{:S(2)}, u32[]{:S(2)}) collective-permute-start(bf16[16,768]{1,0:T(8,128)(2,1)S(1)} %get-tuple-element.60), channel_id=1, source_target_pairs={{0,8},{1,9},{2,10},{3,11},{4,12},{5,13},{6,14},{7,15},{8,0},{9,1},... | collective-permute-start | bytes 73736 | tf_op jit(solution)/shard_map/ppermute | solution.py:481
  6.3 1.3 %collective-permute-start.3 = (bf16[16,768]{1,0:T(8,128)(2,1)S(1)}, bf16[16,768]{1,0:T(8,128)(2,1)S(1)}, u32[]{:S(2)}, u32[]{:S(2)}) collective-permute-start(bf16[16,768]{1,0:T(8,128)(2,1)S(1)} %get-tuple-element.61), channel_id=1, source_target_pairs={{0,12},{1,13},{2,14},{3,15},{4,0},{5,1},{6,2},{7,3},{8,4},{9,5},{1... | collective-permute-start | bytes 73736 | tf_op jit(solution)/shard_map/ppermute | solution.py:481
  7.7 0.9 copy-done
  8.5 0.7 copy-done.2
  9.2 0.7 copy-done.3
  9.8 15.1 %conv_norm.1 = (bf16[49,32,768]{2,1,0:T(8,128)(2,1)S(1)}, f32[32,768]{1,0:T(8,128)S(1)}, bf16[32,64]{1,0:T(8,128)(2,1)S(1)}, bf16[32,64]{1,0:T(8,128)(2,1)S(1)},...) custom-call(s32[1,16]{1,0:T(1,128)S(1)} %copy-done.2, ...), custom_call_target="tpu_custom_call" | custom-call | flops 1000 | bytes 1000 | tf_op jit(solution)/shard_map/conv_norm/pallas_call | solution.py:142
  25.0 0.1 collective-permute-start
  25.1 0.0 collective-permute-done.2.refs_2_
  25.1 0.0 collective-permute-done.3.refs_3_
  25.1 0.1 regroup_rows.1
  25.3 2.0 %collective-permute-start.4 = (bf16[16,768]{1,0:T(8,128)(2,1)S(1)}, bf16[16,768]{1,0:T(8,128)(2,1)S(1)}, u32[]{:S(2)}, u32[]{:S(2)}) collective-permute-start(bf16[16,768]{1,0:T(8,128)(2,1)S(1)} %get-tuple-element.72), channel_id=1, source_target_pairs={{0,1},{1,2},{2,3},{3,0},{4,5},{5,6},{6,7},{7,4},{8,9},{9,10},{10,1... | collective-permute-start | bytes 73736 | tf_op jit(solution)/shard_map/ppermute | solution.py:481
  27.3 3.6 %collective-permute-start.5 = (bf16[16,768]{1,0:T(8,128)(2,1)S(1)}, bf16[16,768]{1,0:T(8,128)(2,1)S(1)}, u32[]{:S(2)}, u32[]{:S(2)}) collective-permute-start(bf16[16,768]{1,0:T(8,128)(2,1)S(1)} %get-tuple-element.73), channel_id=1, source_target_pairs={{0,2},{1,3},{2,0},{3,1},{4,6},{5,7},{6,4},{7,5},{8,10},{9,11},{10,... | collective-permute-start | bytes 73736 | tf_op jit(solution)/shard_map/ppermute | solution.py:481
  30.8 1.0 %collective-permute-start.6 = (bf16[16,768]{1,0:T(8,128)(2,1)S(1)}, bf16[16,768]{1,0:T(8,128)(2,1)S(1)}, u32[]{:S(2)}, u32[]{:S(2)}) collective-permute-start(bf16[16,768]{1,0:T(8,128)(2,1)S(1)} %get-tuple-element.74), channel_id=1, source_target_pairs={{0,3},{1,0},{2,1},{3,2},{4,7},{5,4},{6,5},{7,6},{8,11},{9,8},{10,9... | collective-permute-start | bytes 73736 | tf_op jit(solution)/shard_map/ppermute | solution.py:481
  31.8 0.0 collective-permute-done.4.refs_1_
  31.8 1.1 %collective-permute-done.5.refs_2_ = bf16[16,768]{1,0:T(8,128)(2,1)S(1)} collective-permute-done((bf16[16,768]{1,0:T(8,128)(2,1)S(1)}, bf16[16,768]{1,0:T(8,128)(2,1)S(1)}, u32[]{:S(2)}, u32[]{:S(2)}) %collective-permute-start.5) | collective-permute-done | bytes 24608 | tf_op jit(solution)/shard_map/ppermute | solution.py:481
  32.9 1.7 %collective-permute-done.6.refs_3_ = bf16[16,768]{1,0:T(8,128)(2,1)S(1)} collective-permute-done((bf16[16,768]{1,0:T(8,128)(2,1)S(1)}, bf16[16,768]{1,0:T(8,128)(2,1)S(1)}, u32[]{:S(2)}, u32[]{:S(2)}) %collective-permute-start.6) | collective-permute-done | bytes 24608 | tf_op jit(solution)/shard_map/ppermute | solution.py:481
  34.7 0.1 slot_rows.1.rest_2_
  34.8 0.1 collective-permute-start.7
  34.9 1.2 %collective-permute-done.7.rest_3_ = bf16[32,768]{1,0:T(8,128)(2,1)S(1)} collective-permute-done((bf16[32,768]{1,0:T(8,128)(2,1)S(1)}, bf16[32,768]{1,0:T(8,128)(2,1)S(1)}, u32[]{:S(2)}, u32[]{:S(2)}) %collective-permute-start.7) | collective-permute-done | bytes 49184 | tf_op jit(solution)/shard_map/ppermute | solution.py:481
  36.1 5.7 %hidden_block.4 = (bf16[480,768]{1,0:T(8,128)(2,1)S(1)}, f32[64,768]{1,0:T(8,128)S(1)}) custom-call(bf16[1568,768]{1,0:T(8,128)(2,1)S(1)} %bitcast.16, bf16[1568,768]{1,0:T(8,128)(2,1)S(1)} %collective-permute-done.rest_1_, bf16[32,768]{1,0:T(8,128)(2,1)S(1)} %slot_rows.1.rest_2_, bf16[32,768]{1,0:T(8,128)(2,1)S(1)} %collective-permute-done.7.rest_3_, ...), custom_call_target="tpu_custom_call" | custom-call | flops 1000 | bytes 1000 | tf_op jit(solution)/shard_map/hidden_block/pallas_call | solution.py:257
  41.8 3.3 %collective-permute-start.8 = (bf16[480,768]{1,0:T(8,128)(2,1)S(1)}, bf16[480,768]{1,0:T(8,128)(2,1)S(1)}, u32[]{:S(2)}, u32[]{:S(2)}) collective-permute-start(bf16[480,768]{1,0:T(8,128)(2,1)S(1)} %get-tuple-element.84), channel_id=1, source_target_pairs={{0,64},{1,65},{2,66},{3,67},{4,68},{5,69},{6,70},{7,71},{8,72},{9,... | collective-permute-start | bytes 2211848 | tf_op jit(solution)/shard_map/ppermute | solution.py:481
  45.1 5.7 %hidden_block.5 = (bf16[480,768]{1,0:T(8,128)(2,1)S(1)}, f32[64,768]{1,0:T(8,128)S(1)}) custom-call(bf16[1568,768]{1,0:T(8,128)(2,1)S(1)} %bitcast.17, bf16[1568,768]{1,0:T(8,128)(2,1)S(1)} %collective-permute-done.rest_1_, bf16[32,768]{1,0:T(8,128)(2,1)S(1)} %slot_rows.1.rest_2_, bf16[32,768]{1,0:T(8,128)(2,1)S(1)} %collective-permute-done.7.rest_3_, ...), custom_call_target="tpu_custom_call" | custom-call | flops 1000 | bytes 1000 | tf_op jit(solution)/shard_map/hidden_block/pallas_call | solution.py:257
  50.7 0.7 collective-permute-start.9
  51.4 5.7 %hidden_block.6 = (bf16[480,768]{1,0:T(8,128)(2,1)S(1)}, f32[64,768]{1,0:T(8,128)S(1)}) custom-call(bf16[1568,768]{1,0:T(8,128)(2,1)S(1)} %bitcast.18, bf16[1568,768]{1,0:T(8,128)(2,1)S(1)} %collective-permute-done.rest_1_, bf16[32,768]{1,0:T(8,128)(2,1)S(1)} %slot_rows.1.rest_2_, bf16[32,768]{1,0:T(8,128)(2,1)S(1)} %collective-permute-done.7.rest_3_, ...), custom_call_target="tpu_custom_call" | custom-call | flops 1000 | bytes 1000 | tf_op jit(solution)/shard_map/hidden_block/pallas_call | solution.py:257
  57.1 2.9 %collective-permute-start.11 = (bf16[480,768]{1,0:T(8,128)(2,1)S(1)}, bf16[480,768]{1,0:T(8,128)(2,1)S(1)}, u32[]{:S(2)}, u32[]{:S(2)}) collective-permute-start(bf16[480,768]{1,0:T(8,128)(2,1)S(1)} %get-tuple-element.92), channel_id=1, source_target_pairs={{0,96},{1,97},{2,98},{3,99},{4,100},{5,101},{6,102},{7,103},{8,104... | collective-permute-start | bytes 2211848 | tf_op jit(solution)/shard_map/ppermute | solution.py:481
  60.0 5.7 %hidden_block.7 = (bf16[480,768]{1,0:T(8,128)(2,1)S(1)}, f32[64,768]{1,0:T(8,128)S(1)}) custom-call(bf16[1568,768]{1,0:T(8,128)(2,1)S(1)} %bitcast.19, bf16[1568,768]{1,0:T(8,128)(2,1)S(1)} %collective-permute-done.rest_1_, bf16[32,768]{1,0:T(8,128)(2,1)S(1)} %slot_rows.1.rest_2_, bf16[32,768]{1,0:T(8,128)(2,1)S(1)} %collective-permute-done.7.rest_3_, ...), custom_call_target="tpu_custom_call" | custom-call | flops 1000 | bytes 1000 | tf_op jit(solution)/shard_map/hidden_block/pallas_call | solution.py:257
  65.7 0.1 collective-permute-start.10
  65.8 1.3 %collective-permute-done.10.other_ref = f32[32,768]{1,0:T(8,128)S(1)} collective-permute-done((f32[32,768]{1,0:T(8,128)S(1)}, f32[32,768]{1,0:T(8,128)S(1)}, u32[]{:S(2)}, u32[]{:S(2)}) %collective-permute-start.10) | collective-permute-done | bytes 98336 | tf_op jit(solution)/shard_map/ppermute | solution.py:481
  67.1 1.9 %collective-permute-done.11.c_ref = bf16[480,768]{1,0:T(8,128)(2,1)S(1)} collective-permute-done((bf16[480,768]{1,0:T(8,128)(2,1)S(1)}, bf16[480,768]{1,0:T(8,128)(2,1)S(1)}, u32[]{:S(2)}, u32[]{:S(2)}) %collective-permute-start.11) | collective-permute-done | bytes 737312 | tf_op jit(solution)/shard_map/ppermute | solution.py:481
  69.0 0.8 combine.1
  69.8 0.1 collective-permute-start.12
  69.9 3.7 %collective-permute-start.13 = (bf16[104,1536]{1,0:T(8,128)(2,1)S(1)}, bf16[104,1536]{1,0:T(8,128)(2,1)S(1)}, u32[]{:S(2)}, u32[]{:S(2)}) collective-permute-start(bf16[104,1536]{1,0:T(8,128)(2,1)S(1)} %get-tuple-element.99), channel_id=1, source_target_pairs={{0,2},{1,3},{2,0},{3,1},{4,6},{5,7},{6,4},{7,5},{8,10},{9,11},{10,... | collective-permute-start | bytes 958472 | tf_op jit(solution)/shard_map/ppermute | solution.py:481
  73.6 0.5 collective-permute-start.14
  74.0 0.7 collective-permute-start.15
  74.7 0.8 collective-permute-start.16
  75.5 3.6 %collective-permute-done.15.rest_4_ = bf16[16,768]{1,0:T(8,128)(2,1)S(1)} collective-permute-done((bf16[16,768]{1,0:T(8,128)(2,1)S(1)}, bf16[16,768]{1,0:T(8,128)(2,1)S(1)}, u32[]{:S(2)}, u32[]{:S(2)}) %collective-permute-start.15) | collective-permute-done | bytes 24608 | tf_op jit(solution)/shard_map/ppermute | solution.py:481
  79.1 1.0 %collective-permute-done.16.rest_5_ = bf16[16,768]{1,0:T(8,128)(2,1)S(1)} collective-permute-done((bf16[16,768]{1,0:T(8,128)(2,1)S(1)}, bf16[16,768]{1,0:T(8,128)(2,1)S(1)}, u32[]{:S(2)}, u32[]{:S(2)}) %collective-permute-start.16) | collective-permute-done | bytes 24608 | tf_op jit(solution)/shard_map/ppermute | solution.py:481
  80.0 2.9 %collective-permute-done.17.rest_6_ = bf16[16,768]{1,0:T(8,128)(2,1)S(1)} collective-permute-done((bf16[16,768]{1,0:T(8,128)(2,1)S(1)}, bf16[16,768]{1,0:T(8,128)(2,1)S(1)}, u32[]{:S(2)}, u32[]{:S(2)}) %collective-permute-start.17) | collective-permute-done | bytes 24608 | tf_op jit(solution)/shard_map/ppermute | solution.py:481
  82.9 0.3 second_sum.1
  83.2 0.2 collective-permute-start.18
  83.5 2.5 %collective-permute-start.19 = (bf16[64,768]{1,0:T(8,128)(2,1)S(1)}, bf16[64,768]{1,0:T(8,128)(2,1)S(1)}, u32[]{:S(2)}, u32[]{:S(2)}) collective-permute-start(bf16[64,768]{1,0:T(8,128)(2,1)S(1)} %get-tuple-element.108), channel_id=1, source_target_pairs={{0,8},{1,9},{2,10},{3,11},{4,12},{5,13},{6,14},{7,15},{8,0},{9,1},... | collective-permute-start | bytes 294920 | tf_op jit(solution)/shard_map/ppermute | solution.py:481
  86.0 0.6 collective-permute-start.20
  86.5 3.6 %collective-permute-done.18.a_ref = bf16[64,768]{1,0:T(8,128)(2,1)S(1)} collective-permute-done((bf16[64,768]{1,0:T(8,128)(2,1)S(1)}, bf16[64,768]{1,0:T(8,128)(2,1)S(1)}, u32[]{:S(2)}, u32[]{:S(2)}) %collective-permute-start.18) | collective-permute-done | bytes 98336 | tf_op jit(solution)/shard_map/ppermute | solution.py:481
  90.2 0.9 collective-permute-done.20.c_ref
  91.1 0.8 last_sum.1
  (15 shorter events, 0.1 us)
Async XLA Ops:
  0.6 0.9 copy-start.1
  1.7 23.4 %collective-permute-start.1 = (bf16[16,768]{1,0:T(8,128)(2,1)S(1)}, bf16[16,768]{1,0:T(8,128)(2,1)S(1)}, u32[]{:S(2)}, u32[]{:S(2)}) collective-permute-start(bf16[16,768]{1,0:T(8,128)(2,1)S(1)} %get-tuple-element.59), channel_id=1, source_target_pairs={{0,4},{1,5},{2,6},{3,7},{4,8},{5,9},{6,10},{7,11},{8,12},{9,13},{1... | collective-permute-start | bytes 73736 | tf_op jit(solution)/shard_map/ppermute | solution.py:481
  3.4 21.7 %collective-permute-start.2 = (bf16[16,768]{1,0:T(8,128)(2,1)S(1)}, bf16[16,768]{1,0:T(8,128)(2,1)S(1)}, u32[]{:S(2)}, u32[]{:S(2)}) collective-permute-start(bf16[16,768]{1,0:T(8,128)(2,1)S(1)} %get-tuple-element.60), channel_id=1, source_target_pairs={{0,8},{1,9},{2,10},{3,11},{4,12},{5,13},{6,14},{7,15},{8,0},{9,1},... | collective-permute-start | bytes 73736 | tf_op jit(solution)/shard_map/ppermute | solution.py:481
  6.3 18.8 %collective-permute-start.3 = (bf16[16,768]{1,0:T(8,128)(2,1)S(1)}, bf16[16,768]{1,0:T(8,128)(2,1)S(1)}, u32[]{:S(2)}, u32[]{:S(2)}) collective-permute-start(bf16[16,768]{1,0:T(8,128)(2,1)S(1)} %get-tuple-element.61), channel_id=1, source_target_pairs={{0,12},{1,13},{2,14},{3,15},{4,0},{5,1},{6,2},{7,3},{8,4},{9,5},{1... | collective-permute-start | bytes 73736 | tf_op jit(solution)/shard_map/ppermute | solution.py:481
  7.6 0.9 copy-start
  8.5 0.7 copy-start.2
  9.2 0.7 copy-start.3
  25.0 11.1 %collective-permute-start = (bf16[1568,768]{1,0:T(8,128)(2,1)S(1)}, bf16[1568,768]{1,0:T(8,128)(2,1)S(1)}, u32[]{:S(2)}, u32[]{:S(2)}) collective-permute-start(bf16[1568,768]{1,0:T(8,128)(2,1)S(1)} %bitcast.15), channel_id=1, source_target_pairs={{0,16},{1,17},{2,18},{3,19},{4,20},{5,21},{6,22},{7,23},{8,24},{9,... | collective-permute-start | bytes 7225352 | tf_op jit(solution)/shard_map/ppermute | solution.py:481
  25.3 6.6 %collective-permute-start.4 = (bf16[16,768]{1,0:T(8,128)(2,1)S(1)}, bf16[16,768]{1,0:T(8,128)(2,1)S(1)}, u32[]{:S(2)}, u32[]{:S(2)}) collective-permute-start(bf16[16,768]{1,0:T(8,128)(2,1)S(1)} %get-tuple-element.72), channel_id=1, source_target_pairs={{0,1},{1,2},{2,3},{3,0},{4,5},{5,6},{6,7},{7,4},{8,9},{9,10},{10,1... | collective-permute-start | bytes 73736 | tf_op jit(solution)/shard_map/ppermute | solution.py:481
  27.3 5.7 %collective-permute-start.5 = (bf16[16,768]{1,0:T(8,128)(2,1)S(1)}, bf16[16,768]{1,0:T(8,128)(2,1)S(1)}, u32[]{:S(2)}, u32[]{:S(2)}) collective-permute-start(bf16[16,768]{1,0:T(8,128)(2,1)S(1)} %get-tuple-element.73), channel_id=1, source_target_pairs={{0,2},{1,3},{2,0},{3,1},{4,6},{5,7},{6,4},{7,5},{8,10},{9,11},{10,... | collective-permute-start | bytes 73736 | tf_op jit(solution)/shard_map/ppermute | solution.py:481
  30.8 3.8 %collective-permute-start.6 = (bf16[16,768]{1,0:T(8,128)(2,1)S(1)}, bf16[16,768]{1,0:T(8,128)(2,1)S(1)}, u32[]{:S(2)}, u32[]{:S(2)}) collective-permute-start(bf16[16,768]{1,0:T(8,128)(2,1)S(1)} %get-tuple-element.74), channel_id=1, source_target_pairs={{0,3},{1,0},{2,1},{3,2},{4,7},{5,4},{6,5},{7,6},{8,11},{9,8},{10,9... | collective-permute-start | bytes 73736 | tf_op jit(solution)/shard_map/ppermute | solution.py:481
  34.8 1.3 %collective-permute-start.7 = (bf16[32,768]{1,0:T(8,128)(2,1)S(1)}, bf16[32,768]{1,0:T(8,128)(2,1)S(1)}, u32[]{:S(2)}, u32[]{:S(2)}) collective-permute-start(bf16[32,768]{1,0:T(8,128)(2,1)S(1)} %slot_rows.1.rest_2_), channel_id=1, source_target_pairs={{0,16},{1,17},{2,18},{3,19},{4,20},{5,21},{6,22},{7,23},{8,24},{9,... | collective-permute-start | bytes 147464 | tf_op jit(solution)/shard_map/ppermute | solution.py:481
  41.8 18.2 %collective-permute-start.8 = (bf16[480,768]{1,0:T(8,128)(2,1)S(1)}, bf16[480,768]{1,0:T(8,128)(2,1)S(1)}, u32[]{:S(2)}, u32[]{:S(2)}) collective-permute-start(bf16[480,768]{1,0:T(8,128)(2,1)S(1)} %get-tuple-element.84), channel_id=1, source_target_pairs={{0,64},{1,65},{2,66},{3,67},{4,68},{5,69},{6,70},{7,71},{8,72},{9,... | collective-permute-start | bytes 2211848 | tf_op jit(solution)/shard_map/ppermute | solution.py:481
  50.7 15.0 %collective-permute-start.9 = (bf16[480,768]{1,0:T(8,128)(2,1)S(1)}, bf16[480,768]{1,0:T(8,128)(2,1)S(1)}, u32[]{:S(2)}, u32[]{:S(2)}) collective-permute-start(bf16[480,768]{1,0:T(8,128)(2,1)S(1)} %get-tuple-element.86), channel_id=1, source_target_pairs={{0,32},{1,33},{2,34},{3,35},{4,36},{5,37},{6,38},{7,39},{8,40},{9,... | collective-permute-start | bytes 2211848 | tf_op jit(solution)/shard_map/ppermute | solution.py:481
  57.1 11.9 %collective-permute-start.11 = (bf16[480,768]{1,0:T(8,128)(2,1)S(1)}, bf16[480,768]{1,0:T(8,128)(2,1)S(1)}, u32[]{:S(2)}, u32[]{:S(2)}) collective-permute-start(bf16[480,768]{1,0:T(8,128)(2,1)S(1)} %get-tuple-element.92), channel_id=1, source_target_pairs={{0,96},{1,97},{2,98},{3,99},{4,100},{5,101},{6,102},{7,103},{8,104... | collective-permute-start | bytes 2211848 | tf_op jit(solution)/shard_map/ppermute | solution.py:481
  65.7 1.4 %collective-permute-start.10 = (f32[32,768]{1,0:T(8,128)S(1)}, f32[32,768]{1,0:T(8,128)S(1)}, u32[]{:S(2)}, u32[]{:S(2)}) collective-permute-start(f32[32,768]{1,0:T(8,128)S(1)} %slice.3), channel_id=1, source_target_pairs={{0,16},{1,17},{2,18},{3,19},{4,20},{5,21},{6,22},{7,23},{8,24},{9,... | collective-permute-start | bytes 294920 | tf_op jit(solution)/shard_map/ppermute | solution.py:481
  69.8 13.1 %collective-permute-start.12 = (bf16[104,1536]{1,0:T(8,128)(2,1)S(1)}, bf16[104,1536]{1,0:T(8,128)(2,1)S(1)}, u32[]{:S(2)}, u32[]{:S(2)}) collective-permute-start(bf16[104,1536]{1,0:T(8,128)(2,1)S(1)} %get-tuple-element.98), channel_id=1, source_target_pairs={{0,1},{1,2},{2,3},{3,0},{4,5},{5,6},{6,7},{7,4},{8,9},{9,10},{10,1... | collective-permute-start | bytes 958472 | tf_op jit(solution)/shard_map/ppermute | solution.py:481
  69.9 13.0 %collective-permute-start.13 = (bf16[104,1536]{1,0:T(8,128)(2,1)S(1)}, bf16[104,1536]{1,0:T(8,128)(2,1)S(1)}, u32[]{:S(2)}, u32[]{:S(2)}) collective-permute-start(bf16[104,1536]{1,0:T(8,128)(2,1)S(1)} %get-tuple-element.99), channel_id=1, source_target_pairs={{0,2},{1,3},{2,0},{3,1},{4,6},{5,7},{6,4},{7,5},{8,10},{9,11},{10,... | collective-permute-start | bytes 958472 | tf_op jit(solution)/shard_map/ppermute | solution.py:481
  73.6 9.3 %collective-permute-start.14 = (bf16[104,1536]{1,0:T(8,128)(2,1)S(1)}, bf16[104,1536]{1,0:T(8,128)(2,1)S(1)}, u32[]{:S(2)}, u32[]{:S(2)}) collective-permute-start(bf16[104,1536]{1,0:T(8,128)(2,1)S(1)} %get-tuple-element.100), channel_id=1, source_target_pairs={{0,3},{1,0},{2,1},{3,2},{4,7},{5,4},{6,5},{7,6},{8,11},{9,8},{10,9... | collective-permute-start | bytes 958472 | tf_op jit(solution)/shard_map/ppermute | solution.py:481
  74.0 5.0 %collective-permute-start.15 = (bf16[16,768]{1,0:T(8,128)(2,1)S(1)}, bf16[16,768]{1,0:T(8,128)(2,1)S(1)}, u32[]{:S(2)}, u32[]{:S(2)}) collective-permute-start(bf16[16,768]{1,0:T(8,128)(2,1)S(1)} %get-tuple-element.102), channel_id=1, source_target_pairs={{0,4},{1,5},{2,6},{3,7},{4,8},{5,9},{6,10},{7,11},{8,12},{9,13},{1... | collective-permute-start | bytes 73736 | tf_op jit(solution)/shard_map/ppermute | solution.py:481
  74.7 5.3 %collective-permute-start.16 = (bf16[16,768]{1,0:T(8,128)(2,1)S(1)}, bf16[16,768]{1,0:T(8,128)(2,1)S(1)}, u32[]{:S(2)}, u32[]{:S(2)}) collective-permute-start(bf16[16,768]{1,0:T(8,128)(2,1)S(1)} %get-tuple-element.103), channel_id=1, source_target_pairs={{0,8},{1,9},{2,10},{3,11},{4,12},{5,13},{6,14},{7,15},{8,0},{9,1},... | collective-permute-start | bytes 73736 | tf_op jit(solution)/shard_map/ppermute | solution.py:481
  79.1 3.8 %collective-permute-start.17 = (bf16[16,768]{1,0:T(8,128)(2,1)S(1)}, bf16[16,768]{1,0:T(8,128)(2,1)S(1)}, u32[]{:S(2)}, u32[]{:S(2)}) collective-permute-start(bf16[16,768]{1,0:T(8,128)(2,1)S(1)} %get-tuple-element.104), channel_id=1, source_target_pairs={{0,12},{1,13},{2,14},{3,15},{4,0},{5,1},{6,2},{7,3},{8,4},{9,5},{1... | collective-permute-start | bytes 73736 | tf_op jit(solution)/shard_map/ppermute | solution.py:481
  83.2 6.9 %collective-permute-start.18 = (bf16[64,768]{1,0:T(8,128)(2,1)S(1)}, bf16[64,768]{1,0:T(8,128)(2,1)S(1)}, u32[]{:S(2)}, u32[]{:S(2)}) collective-permute-start(bf16[64,768]{1,0:T(8,128)(2,1)S(1)} %get-tuple-element.107), channel_id=1, source_target_pairs={{0,4},{1,5},{2,6},{3,7},{4,8},{5,9},{6,10},{7,11},{8,12},{9,13},{1... | collective-permute-start | bytes 294920 | tf_op jit(solution)/shard_map/ppermute | solution.py:481
  83.5 6.7 %collective-permute-start.19 = (bf16[64,768]{1,0:T(8,128)(2,1)S(1)}, bf16[64,768]{1,0:T(8,128)(2,1)S(1)}, u32[]{:S(2)}, u32[]{:S(2)}) collective-permute-start(bf16[64,768]{1,0:T(8,128)(2,1)S(1)} %get-tuple-element.108), channel_id=1, source_target_pairs={{0,8},{1,9},{2,10},{3,11},{4,12},{5,13},{6,14},{7,15},{8,0},{9,1},... | collective-permute-start | bytes 294920 | tf_op jit(solution)/shard_map/ppermute | solution.py:481
  86.0 5.1 %collective-permute-start.20 = (bf16[64,768]{1,0:T(8,128)(2,1)S(1)}, bf16[64,768]{1,0:T(8,128)(2,1)S(1)}, u32[]{:S(2)}, u32[]{:S(2)}) collective-permute-start(bf16[64,768]{1,0:T(8,128)(2,1)S(1)} %get-tuple-element.109), channel_id=1, source_target_pairs={{0,12},{1,13},{2,14},{3,15},{4,0},{5,1},{6,2},{7,3},{8,4},{9,5},{1... | collective-permute-start | bytes 294920 | tf_op jit(solution)/shard_map/ppermute | solution.py:481

commit v2 on v1

--- a/solution.py
+++ b/solution.py
@@ -43,7 +43,7 @@
     live = lax.broadcasted_iota(jnp.int32, (tiles, 1), 0) < count
     pick = lambda index, size, on: jnp.where(row_hits(index, size) & on, 1.0, 0.0).astype(jnp.bfloat16)
     hops_y, hops_z = ((owners >> 2) - y) & 3, ((owners & 3) - z) & 3
-    table_ref[...] = pick(((4 - hops_z) & 3) * 16 + ((4 - hops_y) & 3) * 3 + rank, 64, live)
+    table_ref[...] = pick(rank * lanes + owners, table_ref.shape[1], live)
     one, two = (hops_z, hops_y), (hops_y, hops_z)
     near, far = [jnp.where(core == 0, p, q) for p, q in zip(one, two)]
     send_ref[...] = pick(near * 16 + far * 3 + rank, 64, live)
@@ -144,7 +144,7 @@
         out_shape=(
             shape((cells, tiles, width), jnp.bfloat16),
             shape((tiles, width), jnp.float32),
-            shape((tiles, 64), jnp.bfloat16),
+            shape((tiles, 16 * capacity), jnp.bfloat16),
             shape((tiles, 64), jnp.bfloat16),
             shape((16 * capacity, 64), jnp.bfloat16),
             *[shape((units, width), jnp.bfloat16)] * 8,
@@ -180,12 +180,12 @@
     up = up_s[...]
     both = jnp.concatenate([sg[...] for sg in sgs for _ in range(128 // tiles)], axis=0)
     dh_both = f32_dot(dn_s[...], both, nt) * scale
-    dh = [dh_both[:, 0:128], dh_both[:, 128:256]]
+    dh = [dh_both[:, 128 * p : 128 * p + 128] for p in range(2)]
 
     runs, tails = [], []
     for p, ref in enumerate(parts):
         full = ref.shape[0] // 256 * 256
-        runs.append((p, full))
+        runs += [(p, at, min(at + 512, full)) for at in range(0, full, 512)]
         for cut in range(full, ref.shape[0], 128):
             tails.append((p, cut, min(128, ref.shape[0] - cut)))
     tails.sort(key=lambda t: -t[2])
@@ -210,14 +210,14 @@
         term = f32_dot(grads[:, start : start + size], rhs())
         return term if up_rows is None else up_rows + term
 
-    for p, full in runs:
+    for p, low, high in runs:
         start = column
-        for cut in range(0, full, 256):
+        for cut in range(low, high, 256):
             tile(parts[p][cut : cut + 256, :], [(p, 128)] * 2, column)
             column += 256
         if waiting is not None:
             up_rows = absorb(waiting, up_rows)
-        waiting = (start, full, lambda p=p, full=full: parts[p][0:full, :])
+        waiting = (start, high - low, lambda p=p, low=low, high=high: parts[p][low:high, :])
     start = column
     group, size = [], 0
     for n, (p, cut, w) in enumerate(tails):
@@ -231,8 +231,6 @@
     up_rows = absorb(waiting, up_rows)
     rhs = jnp.concatenate([parts[p][c : c + w, :] for p, c, w in tails], axis=0)
     up_rows = absorb((start, column - start, lambda: rhs), up_rows)
-    pay_ref[0:units] = up_rows.astype(jnp.bfloat16)
-
     pick = (
         lax.broadcasted_iota(jnp.int32, (tiles, 128), 0)
         == lax.broadcasted_iota(jnp.int32, (tiles, 128), 1)
@@ -244,6 +242,7 @@
             value = value + pltpu.roll(value, shift, 1)
             shift //= 2
         flat.append(f32_dot(pick, (value * scale).astype(jnp.bfloat16), nt).astype(jnp.bfloat16))
+    pay_ref[0:units] = up_rows.astype(jnp.bfloat16)
     emb_out[...] = emb_ref[...] + f32_dot(jnp.concatenate(flat, axis=0), dn_s[...])
     for h in range(2):
         pay_ref[units + h * tiles : units + (h + 1) * tiles] = sgs[h][...]
@@ -282,13 +281,10 @@
     return f32_dot(one_hot_rows(target, 64), jnp.concatenate(blocks, axis=0))
 
 
-def spread_kernel(grad_ref, *outs):
-    enc = lax.axis_index("enc")
-    y, z = enc // 4, enc % 4
-    col = lax.broadcasted_iota(jnp.int32, (1, grad_ref.shape[0]), 1)
-    reader = col & 15
-    target = (((reader >> 2) - y) & 3) * 16 + (((reader & 3) - z) & 3) * 3 + (col >> 4)
-    rows = f32_dot(one_hot_rows(target, 64), grad_ref[...]).astype(jnp.bfloat16)
+def embed_kernel(table_ref, mean_ref, emb_ref, other_ref, *outs):
+    tiles = mean_ref.shape[0]
+    embed = (mean_ref[...] + emb_ref[0:tiles] + other_ref[...]).astype(jnp.bfloat16)
+    rows = f32_dot(table_ref[...], embed, tn).astype(jnp.bfloat16)
     for k, out in enumerate(outs):
         out[...] = rows[16 * k : 16 * k + 16]
 
@@ -299,46 +295,35 @@
         out[...] = rows[16 * k : 16 * k + 16]
 
 
-def slot_kernel(table_ref, *refs):
-    rows = jnp.concatenate([r[...] for r in refs[0:4]], axis=0)
-    refs[4][...] = f32_dot(table_ref[...], rows).astype(jnp.bfloat16)
-
-
-def small_call(kernel, name, args, shapes, cost):
+def small_call(kernel, name, args, width, cost):
     return pl.pallas_call(
         kernel,
-        out_shape=tuple(jax.ShapeDtypeStruct(dims, jnp.bfloat16) for dims in shapes),
+        out_shape=(jax.ShapeDtypeStruct((16, width), jnp.bfloat16),) * 4,
         in_specs=[VMEM] * len(args),
-        out_specs=(VMEM,) * len(shapes),
+        out_specs=(VMEM,) * 4,
         compiler_params=pltpu.CompilerParams(vmem_limit_bytes=4 << 20),
         cost_estimate=cost,
         name=name,
     )(*args)
 
 
-def spread_rows(grads):
-    return small_call(spread_kernel, "spread_rows", (grads,), [(16, grads.shape[1])] * 4, small_cost)
+def embed_rows(table, mean, emb, other):
+    args = (table, mean, emb, other)
+    return small_call(embed_kernel, "embed_rows", args, mean.shape[1], small_cost)
 
 
 def regroup_rows(blocks):
-    return small_call(regroup_kernel, "regroup_rows", blocks, [blocks[0].shape] * 4, large_cost)
-
-
-def slot_rows(table, blocks):
-    dims = (table.shape[0], blocks[0].shape[1])
-    return small_call(slot_kernel, "slot_rows", (table, *blocks), [dims], large_cost)[0]
-
-
-def combine_kernel(a_ref, b_ref, c_ref, d_ref, table_ref, mean_ref, emb_ref, other_ref, *outs):
-    pays, own_out, embeds, total = outs[0:3], outs[3], outs[4:8], outs[8]
+    return small_call(regroup_kernel, "regroup_rows", blocks, blocks[0].shape[1], large_cost)
+
+
+def combine_kernel(a_ref, b_ref, c_ref, d_ref, *outs):
+    total = outs[4]
     slide, enc = lax.axis_index("slide"), lax.axis_index("enc")
     x, core, z = slide // 2, slide % 2, enc % 4
     units = total.shape[0]
     width = a_ref.shape[1]
     tiles = (a_ref.shape[0] - units) // 3
     refs = (a_ref, b_ref, c_ref, d_ref)
-    embed = (mean_ref[...] + emb_ref[0:tiles] + other_ref[...]).astype(jnp.bfloat16)
-    rows = f32_dot(table_ref[...], embed, tn)
     up = None
     for r in refs:
         term = r[0:units].astype(jnp.float32)
@@ -358,63 +343,45 @@
             on_x = ((x + hop) & 3) * sub + i * last
             start = pl.multiple_of(jnp.where(core == 0, on_z, on_x), 8)
             pieces.append(total[pl.ds(start, last), :])
-        mine = rows[16 * hop : 16 * hop + 16]
-        embeds[hop][...] = mine.astype(jnp.bfloat16)
-        if hop:
-            pieces.append(jnp.concatenate([mine[0:8], mine[8:16]], axis=1))
-            pays[hop - 1][...] = jnp.concatenate(pieces, axis=0).astype(jnp.bfloat16)
-        else:
-            own_out[...] = jnp.concatenate(pieces, axis=0)
-
-
-def combine(payloads, units, table, mean, emb, other):
+        out = outs[(hop + 3) % 4]
+        out[...] = jnp.concatenate(pieces, axis=0).astype(out.dtype)
+
+
+def combine(payloads, units):
     width = payloads[0].shape[1]
-    shape = jax.ShapeDtypeStruct
+    shape = lambda dtype: jax.ShapeDtypeStruct((units // 4, 2 * width), dtype)
     return pl.pallas_call(
         combine_kernel,
-        out_shape=(
-            *[shape((units // 4 + 8, 2 * width), jnp.bfloat16)] * 3,
-            shape((units // 4, 2 * width), jnp.float32),
-            *[shape((16, width), jnp.bfloat16)] * 4,
-        ),
-        in_specs=[VMEM] * 8,
-        out_specs=(VMEM,) * 8,
+        out_shape=(shape(jnp.bfloat16),) * 3 + (shape(jnp.float32),),
+        in_specs=[VMEM] * 4,
+        out_specs=(VMEM,) * 4,
         scratch_shapes=[pltpu.VMEM((units, 2 * width), jnp.float32)],
         compiler_params=pltpu.CompilerParams(vmem_limit_bytes=16 << 20),
         cost_estimate=small_cost,
         name="combine",
-    )(*payloads, table, mean, emb, other)
+    )(*payloads)
 
 
 def second_kernel(own_ref, *rest):
-    received, own_embed, moved = rest[0:3], rest[3], rest[4:7]
-    own_out, pays, embed_out, total = rest[7], rest[8:11], rest[11], rest[12]
+    received, embeds = rest[0:3], rest[3:6]
+    own_out, pays, total = rest[6], rest[7:10], rest[10]
     core, enc = lax.axis_index("slide") % 2, lax.axis_index("enc")
     third = jnp.where(core == 0, enc // 4, enc % 4)
     width = own_out.shape[1]
-    sub = own_ref.shape[0]
-    last = sub // 4
-    received = [r[...].astype(jnp.float32) for r in received]
-    total[...] = own_ref[...] + sum(r[0:sub] for r in received)
-    blocks = [own_embed[...]]
-    for r, other in zip(received, moved):
-        ridden = jnp.concatenate([r[sub:, 0:width], r[sub:, width : 2 * width]], axis=0)
-        block = jnp.where(core == 0, ridden, other[...].astype(jnp.float32))
-        blocks.append(block.astype(jnp.bfloat16))
-    embeds = regroup(blocks)
+    last = own_ref.shape[0] // 4
+    total[...] = own_ref[...] + sum(r[...].astype(jnp.float32) for r in received)
     for hop in range(4):
         rows = pl.ds(pl.multiple_of(((third + hop) & 3) * last, 8), last)
         up, down = total[rows, 0:width], total[rows, width : 2 * width]
         if hop == 0:
             own_out[...] = jnp.concatenate([up, down], axis=0)
-            embed_out[...] = embeds[0:16].astype(jnp.bfloat16)
         else:
             pays[hop - 1][...] = jnp.concatenate(
-                [up, down, embeds[16 * hop : 16 * hop + 16]], axis=0
+                [up, down, embeds[hop - 1][...].astype(jnp.float32)], axis=0
             ).astype(jnp.bfloat16)
 
 
-def second_sum(own, received, own_embed, moved):
+def second_sum(own, received, embeds):
     sub, width = own.shape[0], own.shape[1] // 2
     rows = sub // 2
     return pl.pallas_call(
@@ -422,15 +389,14 @@
         out_shape=(
             jax.ShapeDtypeStruct((rows, width), jnp.float32),
             *[jax.ShapeDtypeStruct((rows + 16, width), jnp.bfloat16)] * 3,
-            jax.ShapeDtypeStruct((16, width), jnp.bfloat16),
         ),
-        in_specs=[VMEM] * 8,
-        out_specs=(VMEM,) * 5,
+        in_specs=[VMEM] * 7,
+        out_specs=(VMEM,) * 4,
         scratch_shapes=[pltpu.VMEM(own.shape, jnp.float32)],
         compiler_params=pltpu.CompilerParams(vmem_limit_bytes=8 << 20),
         cost_estimate=small_cost,
         name="second_sum",
-    )(own, *received, own_embed, *moved)
+    )(own, *received, *embeds)
 
 
 def last_kernel(place_ref, own_ref, embed_ref, a_ref, b_ref, c_ref, up_ref, down_ref, out_ref):
@@ -465,7 +431,7 @@
 
 
 def move(value, stage, hop):
-    spots = {0: (1, 1), 1: (0, 2), 2: (3, 0), 3: (2, 3), 4: (2, 2), 5: (3, 3)}[stage]
+    spots = {0: (1, 1), 1: (0, 2), 2: (3, 0), 3: (2, 3), 4: (3, 2)}[stage]
     pairs = []
     for x in range(4):
         for core in range(2):
@@ -488,18 +454,15 @@
     units = up_weight.shape[0] // 8
     capacity = embed_grad.shape[3]
 
-    sent = spread_rows(jnp.transpose(embed_grad[0, 0], (1, 0, 2)).reshape(-1, width))
-    arrived = [move(sent[hop], 4, hop) for hop in (1, 2, 3)]
-    tissue_counts, sent = lax.optimization_barrier((tissue_counts, sent))
+    fetched = lax.all_to_all(
+        jnp.transpose(embed_grad[0, 0], (1, 0, 2)), "enc", split_axis=1, concat_axis=1, tiled=True
+    )
     normed, map_mean, table, send_table, place, *weights = conv_norm(
         tissue_counts, tile_owner, maps, depth_kernel, up_weight, down_weight, capacity
     )
     normed = normed.reshape(-1, width)
     sib_normed = move(normed, 0, 0)
-    table, arrived = lax.optimization_barrier((table, arrived))
-    sent = regroup_rows((sent[0], *arrived))
-    arrived = [move(sent[hop], 5, hop) for hop in (1, 2, 3)]
-    slot_grad = slot_rows(table, (sent[0], *arrived))
+    slot_grad = f32_dot(table, fetched.reshape(capacity * lane_count, width)).astype(jnp.bfloat16)
     sib_grad = move(slot_grad, 0, 0)
 
     emb = jnp.zeros((2 * tiles, width), jnp.float32)
@@ -514,12 +477,13 @@
 
     other_emb = move(emb[tiles:], 0, 0)
     payloads[1], other_emb = lax.optimization_barrier((payloads[1], other_emb))
-    *pays, own, own_embed, embed_1, embed_2, embed_3 = combine(
-        payloads, units, send_table, map_mean, emb, other_emb
-    )
+    rows_out = embed_rows(send_table, map_mean, emb, other_emb)
+    payloads, _ = lax.optimization_barrier((payloads, rows_out))
+    *pays, own = combine(payloads, units)
     received = [move(pays[hop - 1], 2, hop) for hop in (1, 2, 3)]
-    moved = [move(rows, 4, hop) for hop, rows in ((1, embed_1), (2, embed_2), (3, embed_3))]
-    own, *pays, own_embed = second_sum(own, received, own_embed, moved)
+    moved = [move(rows_out[hop], 4, hop) for hop in (1, 2, 3)]
+    own_embed, *embeds = regroup_rows((rows_out[0], *moved))
+    own, *pays = second_sum(own, received, embeds)
     by_hop = {hop: move(pays[hop - 1], 3, hop) for hop in (1, 2, 3)}
     up_part, down_part, arrived = last_sum(
         place, own, own_embed, [by_hop[hop] for hop in (1, 2, 3)]

time: 92.9 us -> 91.7 us (0.987)
  blocking collectives: 0 us -> 15.7 us
  starting transfers between devices: 28.7 us -> 20 us
  waiting for transfers between devices: 19.2 us -> 13.5 us
  Pallas kernels: 40.1 us -> 39.1 us
    all_to_all x0 -> x1, blocking collectives: none -> 15.7 us  [body(): lax.all_to_all(jnp.transpose(embed_grad[0, 0], (1, 0, 2)), 'enc', split_a...]
    ppermute x21 -> x15, starting transfers between devices: 28.7 us -> 20 us  [move(): return lax.ppermute(value, axes, pairs)]
    ppermute x21 -> x15, waiting for transfers between devices: 19.2 us -> 13.5 us  [move(): return lax.ppermute(value, axes, pairs)]
    unnamed x8 -> x9, local copies, waits for them, and re-layouts: 3.07 us -> 2.25 us
  transfers between devices with their start and end apart: 21 -> 15, of which waited for: 10 -> 6; matrix products, arithmetic and copies ran while one was open for 0% -> 0% of each run, Pallas kernels for 35% -> 19%
where the time goes in v2:
time: 91.7 us; the launch traced here: 91.5 us
  Pallas kernels  39.1 us (43%)
  starting transfers between devices  20 us (22%)
  blocking collectives  15.7 us (17%)
  waiting for transfers between devices  13.5 us (15%)
  local copies, waits for them, and re-layouts  2.28 us (2%)
    pallas_call x4, Pallas kernels, hidden_block(): pl.pallas_call(block_kernel, out_shape=(jax.ShapeDtypeStruct((units + 3 *...  21.8 us
    ppermute x15, starting transfers between devices, move(): return lax.ppermute(value, axes, pairs)  20 us
    all_to_all x1, blocking collectives, body(): lax.all_to_all(jnp.transpose(embed_grad[0, 0], (1, 0, 2)), 'enc', split_a...  15.7 us
    pallas_call x1, Pallas kernels, conv_norm(): pl.pallas_call(conv_kernel, out_shape=(shape((cells, tiles, width), jnp.b...  15.1 us
    ppermute x15, waiting for transfers between devices, move(): return lax.ppermute(value, axes, pairs)  13.5 us
    unnamed x9, local copies, waits for them, and re-layouts  2.25 us
  transfers between devices with their start and end apart: 15, of which 6 were waited for; matrix products, arithmetic and copies ran while one was open for 0% of the time, Pallas kernels for 19%

profile of v2, /device:TPU:0, one launch (start us, length us, event | category | flops | bytes accessed | tf_op | source)
XLA Modules:
  0.0 91.5 jit_solution(17807892152320102440)
XLA Ops:
  0.6 0.0 copy-start
  0.6 0.9 copy-done
  1.5 0.7 copy-done.1
  2.2 0.7 copy-done.2
  2.8 15.1 %conv_norm.1 = (bf16[49,32,768]{2,1,0:T(8,128)(2,1)S(1)}, f32[32,768]{1,0:T(8,128)S(1)}, bf16[32,48]{1,0:T(8,128)(2,1)S(1)}, bf16[32,64]{1,0:T(8,128)(2,1)S(1)},...) custom-call(s32[1,16]{1,0:T(1,128)S(1)} %copy-done.1, ...), custom_call_target="tpu_custom_call" | custom-call | flops 1000 | bytes 1000 | tf_op jit(solution)/shard_map/conv_norm/pallas_call | solution.py:142
  18.0 0.1 collective-permute-start
  18.1 0.0 copy-done.3
  18.1 0.1 copy.14
  18.1 15.7 %all_to_all.5 = bf16[3,16,768]{2,0,1:T(4,128)(2,1)S(1)} all-to-all(bf16[3,16,768]{2,0,1:T(4,128)(2,1)S(1)} %bitcast.25), channel_id=1, replica_groups=mesh['slide'=8,'enc'=16] {'enc'}, dimensions={1} | all-to-all | bytes 147456 | tf_op jit(solution)/shard_map/all_to_all | solution.py:457
  33.8 0.1 convolution_convert_fusion.rest_2_
  34.0 0.1 collective-permute-start.1
  34.1 1.2 %collective-permute-done.1.rest_3_ = bf16[32,768]{1,0:T(8,128)(2,1)S(1)} collective-permute-done((bf16[32,768]{1,0:T(8,128)(2,1)S(1)}, bf16[32,768]{1,0:T(8,128)(2,1)S(1)}, u32[]{:S(2)}, u32[]{:S(2)}) %collective-permute-start.1) | collective-permute-done | bytes 49184 | tf_op jit(solution)/shard_map/ppermute | solution.py:447
  35.3 0.0 collective-permute-done.rest_1_
  35.3 5.4 %hidden_block.4 = (bf16[480,768]{1,0:T(8,128)(2,1)S(1)}, f32[64,768]{1,0:T(8,128)S(1)}) custom-call(bf16[1568,768]{1,0:T(8,128)(2,1)S(1)} %bitcast.19, bf16[1568,768]{1,0:T(8,128)(2,1)S(1)} %collective-permute-done.rest_1_, bf16[32,768]{1,0:T(8,128)(2,1)S(1)} %convolution_convert_fusion.rest_2_, bf16[32,768]{1,0:T(8,128)(2,1)S(1)} %collective-permute-done.1.rest_3_, ...), custom_call_target="tpu_custom_call" | custom-call | flops 1000 | bytes 1000 | tf_op jit(solution)/shard_map/hidden_block/pallas_call | solution.py:256
  40.8 3.3 %collective-permute-start.2 = (bf16[480,768]{1,0:T(8,128)(2,1)S(1)}, bf16[480,768]{1,0:T(8,128)(2,1)S(1)}, u32[]{:S(2)}, u32[]{:S(2)}) collective-permute-start(bf16[480,768]{1,0:T(8,128)(2,1)S(1)} %get-tuple-element.63), channel_id=1, source_target_pairs={{0,64},{1,65},{2,66},{3,67},{4,68},{5,69},{6,70},{7,71},{8,72},{9,... | collective-permute-start | bytes 2211848 | tf_op jit(solution)/shard_map/ppermute | solution.py:447
  44.0 5.4 %hidden_block.5 = (bf16[480,768]{1,0:T(8,128)(2,1)S(1)}, f32[64,768]{1,0:T(8,128)S(1)}) custom-call(bf16[1568,768]{1,0:T(8,128)(2,1)S(1)} %bitcast.20, bf16[1568,768]{1,0:T(8,128)(2,1)S(1)} %collective-permute-done.rest_1_, bf16[32,768]{1,0:T(8,128)(2,1)S(1)} %convolution_convert_fusion.rest_2_, bf16[32,768]{1,0:T(8,128)(2,1)S(1)} %collective-permute-done.1.rest_3_, ...), custom_call_target="tpu_custom_call" | custom-call | flops 1000 | bytes 1000 | tf_op jit(solution)/shard_map/hidden_block/pallas_call | solution.py:256
  49.5 0.7 collective-permute-start.3
  50.2 5.4 %hidden_block.6 = (bf16[480,768]{1,0:T(8,128)(2,1)S(1)}, f32[64,768]{1,0:T(8,128)S(1)}) custom-call(bf16[1568,768]{1,0:T(8,128)(2,1)S(1)} %bitcast.21, bf16[1568,768]{1,0:T(8,128)(2,1)S(1)} %collective-permute-done.rest_1_, bf16[32,768]{1,0:T(8,128)(2,1)S(1)} %convolution_convert_fusion.rest_2_, bf16[32,768]{1,0:T(8,128)(2,1)S(1)} %collective-permute-done.1.rest_3_, ...), custom_call_target="tpu_custom_call" | custom-call | flops 1000 | bytes 1000 | tf_op jit(solution)/shard_map/hidden_block/pallas_call | solution.py:256
  55.6 2.9 %collective-permute-start.5 = (bf16[480,768]{1,0:T(8,128)(2,1)S(1)}, bf16[480,768]{1,0:T(8,128)(2,1)S(1)}, u32[]{:S(2)}, u32[]{:S(2)}) collective-permute-start(bf16[480,768]{1,0:T(8,128)(2,1)S(1)} %get-tuple-element.71), channel_id=1, source_target_pairs={{0,96},{1,97},{2,98},{3,99},{4,100},{5,101},{6,102},{7,103},{8,104... | collective-permute-start | bytes 2211848 | tf_op jit(solution)/shard_map/ppermute | solution.py:447
  58.5 0.0 collective-permute-done.2.a_ref
  58.5 5.4 %hidden_block.7 = (bf16[480,768]{1,0:T(8,128)(2,1)S(1)}, f32[64,768]{1,0:T(8,128)S(1)}) custom-call(bf16[1568,768]{1,0:T(8,128)(2,1)S(1)} %bitcast.22, bf16[1568,768]{1,0:T(8,128)(2,1)S(1)} %collective-permute-done.rest_1_, bf16[32,768]{1,0:T(8,128)(2,1)S(1)} %convolution_convert_fusion.rest_2_, bf16[32,768]{1,0:T(8,128)(2,1)S(1)} %collective-permute-done.1.rest_3_, ...), custom_call_target="tpu_custom_call" | custom-call | flops 1000 | bytes 1000 | tf_op jit(solution)/shard_map/hidden_block/pallas_call | solution.py:256
  64.0 0.1 collective-permute-start.4
  64.1 0.0 collective-permute-done.3.b_ref
  64.1 1.3 %collective-permute-done.4.other_ref = f32[32,768]{1,0:T(8,128)S(1)} collective-permute-done((f32[32,768]{1,0:T(8,128)S(1)}, f32[32,768]{1,0:T(8,128)S(1)}, u32[]{:S(2)}, u32[]{:S(2)}) %collective-permute-start.4) | collective-permute-done | bytes 98336 | tf_op jit(solution)/shard_map/ppermute | solution.py:447
  65.4 0.2 embed_rows.1
  65.6 0.6 collective-permute-start.9
  66.2 2.2 %collective-permute-start.10 = (bf16[16,768]{1,0:T(8,128)(2,1)S(1)}, bf16[16,768]{1,0:T(8,128)(2,1)S(1)}, u32[]{:S(2)}, u32[]{:S(2)}) collective-permute-start(bf16[16,768]{1,0:T(8,128)(2,1)S(1)} %get-tuple-element.78), channel_id=1, source_target_pairs={{0,2},{1,3},{2,0},{3,1},{4,6},{5,7},{6,4},{7,5},{8,10},{9,11},{10,... | collective-permute-start | bytes 73736 | tf_op jit(solution)/shard_map/ppermute | solution.py:447
  68.4 1.4 %collective-permute-start.11 = (bf16[16,768]{1,0:T(8,128)(2,1)S(1)}, bf16[16,768]{1,0:T(8,128)(2,1)S(1)}, u32[]{:S(2)}, u32[]{:S(2)}) collective-permute-start(bf16[16,768]{1,0:T(8,128)(2,1)S(1)} %get-tuple-element.79), channel_id=1, source_target_pairs={{0,3},{1,0},{2,1},{3,2},{4,7},{5,4},{6,5},{7,6},{8,11},{9,8},{10,9... | collective-permute-start | bytes 73736 | tf_op jit(solution)/shard_map/ppermute | solution.py:447
  69.7 0.0 collective-permute-done.5.c_ref
  69.8 0.8 combine.1
  70.6 0.7 collective-permute-start.6
  71.3 1.5 %collective-permute-start.7 = (bf16[96,1536]{1,0:T(8,128)(2,1)S(1)}, bf16[96,1536]{1,0:T(8,128)(2,1)S(1)}, u32[]{:S(2)}, u32[]{:S(2)}) collective-permute-start(bf16[96,1536]{1,0:T(8,128)(2,1)S(1)} %get-tuple-element.86), channel_id=1, source_target_pairs={{0,2},{1,3},{2,0},{3,1},{4,6},{5,7},{6,4},{7,5},{8,10},{9,11},{10,... | collective-permute-start | bytes 884744 | tf_op jit(solution)/shard_map/ppermute | solution.py:447
  72.8 0.0 collective-permute-done.9.refs_1_
  72.8 2.5 %collective-permute-start.8 = (bf16[96,1536]{1,0:T(8,128)(2,1)S(1)}, bf16[96,1536]{1,0:T(8,128)(2,1)S(1)}, u32[]{:S(2)}, u32[]{:S(2)}) collective-permute-start(bf16[96,1536]{1,0:T(8,128)(2,1)S(1)} %get-tuple-element.87), channel_id=1, source_target_pairs={{0,3},{1,0},{2,1},{3,2},{4,7},{5,4},{6,5},{7,6},{8,11},{9,8},{10,9... | collective-permute-start | bytes 884744 | tf_op jit(solution)/shard_map/ppermute | solution.py:447
  75.3 0.0 collective-permute-done.10.refs_2_
  75.3 0.0 collective-permute-done.11.refs_3_
  75.3 0.2 regroup_rows.1
  75.5 6.2 %collective-permute-done.6.rest_0_ = bf16[96,1536]{1,0:T(8,128)(2,1)S(1)} collective-permute-done((bf16[96,1536]{1,0:T(8,128)(2,1)S(1)}, bf16[96,1536]{1,0:T(8,128)(2,1)S(1)}, u32[]{:S(2)}, u32[]{:S(2)}) %collective-permute-start.6) | collective-permute-done | bytes 294944 | tf_op jit(solution)/shard_map/ppermute | solution.py:447
  81.7 0.0 collective-permute-done.7.rest_1_
  81.7 0.9 collective-permute-done.8.rest_2_
  82.6 0.3 second_sum.1
  82.9 0.6 collective-permute-start.12
  83.5 2.1 %collective-permute-start.13 = (bf16[64,768]{1,0:T(8,128)(2,1)S(1)}, bf16[64,768]{1,0:T(8,128)(2,1)S(1)}, u32[]{:S(2)}, u32[]{:S(2)}) collective-permute-start(bf16[64,768]{1,0:T(8,128)(2,1)S(1)} %get-tuple-element.94), channel_id=1, source_target_pairs={{0,8},{1,9},{2,10},{3,11},{4,12},{5,13},{6,14},{7,15},{8,0},{9,1},... | collective-permute-start | bytes 294920 | tf_op jit(solution)/shard_map/ppermute | solution.py:447
  85.5 1.3 %collective-permute-start.14 = (bf16[64,768]{1,0:T(8,128)(2,1)S(1)}, bf16[64,768]{1,0:T(8,128)(2,1)S(1)}, u32[]{:S(2)}, u32[]{:S(2)}) collective-permute-start(bf16[64,768]{1,0:T(8,128)(2,1)S(1)} %get-tuple-element.95), channel_id=1, source_target_pairs={{0,12},{1,13},{2,14},{3,15},{4,0},{5,1},{6,2},{7,3},{8,4},{9,5},{1... | collective-permute-start | bytes 294920 | tf_op jit(solution)/shard_map/ppermute | solution.py:447
  86.8 3.0 %collective-permute-done.12.a_ref = bf16[64,768]{1,0:T(8,128)(2,1)S(1)} collective-permute-done((bf16[64,768]{1,0:T(8,128)(2,1)S(1)}, bf16[64,768]{1,0:T(8,128)(2,1)S(1)}, u32[]{:S(2)}, u32[]{:S(2)}) %collective-permute-start.12) | collective-permute-done | bytes 98336 | tf_op jit(solution)/shard_map/ppermute | solution.py:447
  89.8 0.0 collective-permute-done.13.b_ref
  89.8 0.9 collective-permute-done.14.c_ref
  90.7 0.8 last_sum.1
  (6 shorter events, 0.0 us)
Async XLA Ops:
  0.6 0.9 copy-start
  1.5 0.7 copy-start.1
  2.2 0.7 copy-start.2
  2.8 15.2 %copy-start.3 = (bf16[1,1,16,3,768]{4,2,3,1,0:T(8,128)(2,1)S(1)}, bf16[1,1,16,3,768]{4,2,3,1,0:T(8,128)(2,1)}, u32[]{:S(2)}) copy-start(bf16[1,1,16,3,768]{4,2,3,1,0:T(8,128)(2,1)} %param.10) | copy-start | bytes 221188
  18.0 17.3 %collective-permute-start = (bf16[1568,768]{1,0:T(8,128)(2,1)S(1)}, bf16[1568,768]{1,0:T(8,128)(2,1)S(1)}, u32[]{:S(2)}, u32[]{:S(2)}) collective-permute-start(bf16[1568,768]{1,0:T(8,128)(2,1)S(1)} %bitcast.18), channel_id=1, source_target_pairs={{0,16},{1,17},{2,18},{3,19},{4,20},{5,21},{6,22},{7,23},{8,24},{9,... | collective-permute-start | bytes 7225352 | tf_op jit(solution)/shard_map/ppermute | solution.py:447
  34.0 1.3 %collective-permute-start.1 = (bf16[32,768]{1,0:T(8,128)(2,1)S(1)}, bf16[32,768]{1,0:T(8,128)(2,1)S(1)}, u32[]{:S(2)}, u32[]{:S(2)}) collective-permute-start(bf16[32,768]{1,0:T(8,128)(2,1)S(1)} %convolution_convert_fusion.rest_2_), channel_id=1, source_target_pairs={{0,16},{1,17},{2,18},{3,19},{4,20},{5,21},{6,22},{7,23},{8,24},{9,... | collective-permute-start | bytes 147464 | tf_op jit(solution)/shard_map/ppermute | solution.py:447
  40.8 17.8 %collective-permute-start.2 = (bf16[480,768]{1,0:T(8,128)(2,1)S(1)}, bf16[480,768]{1,0:T(8,128)(2,1)S(1)}, u32[]{:S(2)}, u32[]{:S(2)}) collective-permute-start(bf16[480,768]{1,0:T(8,128)(2,1)S(1)} %get-tuple-element.63), channel_id=1, source_target_pairs={{0,64},{1,65},{2,66},{3,67},{4,68},{5,69},{6,70},{7,71},{8,72},{9,... | collective-permute-start | bytes 2211848 | tf_op jit(solution)/shard_map/ppermute | solution.py:447
  49.5 14.6 %collective-permute-start.3 = (bf16[480,768]{1,0:T(8,128)(2,1)S(1)}, bf16[480,768]{1,0:T(8,128)(2,1)S(1)}, u32[]{:S(2)}, u32[]{:S(2)}) collective-permute-start(bf16[480,768]{1,0:T(8,128)(2,1)S(1)} %get-tuple-element.65), channel_id=1, source_target_pairs={{0,32},{1,33},{2,34},{3,35},{4,36},{5,37},{6,38},{7,39},{8,40},{9,... | collective-permute-start | bytes 2211848 | tf_op jit(solution)/shard_map/ppermute | solution.py:447
  55.6 14.2 %collective-permute-start.5 = (bf16[480,768]{1,0:T(8,128)(2,1)S(1)}, bf16[480,768]{1,0:T(8,128)(2,1)S(1)}, u32[]{:S(2)}, u32[]{:S(2)}) collective-permute-start(bf16[480,768]{1,0:T(8,128)(2,1)S(1)} %get-tuple-element.71), channel_id=1, source_target_pairs={{0,96},{1,97},{2,98},{3,99},{4,100},{5,101},{6,102},{7,103},{8,104... | collective-permute-start | bytes 2211848 | tf_op jit(solution)/shard_map/ppermute | solution.py:447
  64.0 1.4 %collective-permute-start.4 = (f32[32,768]{1,0:T(8,128)S(1)}, f32[32,768]{1,0:T(8,128)S(1)}, u32[]{:S(2)}, u32[]{:S(2)}) collective-permute-start(f32[32,768]{1,0:T(8,128)S(1)} %slice.3), channel_id=1, source_target_pairs={{0,16},{1,17},{2,18},{3,19},{4,20},{5,21},{6,22},{7,23},{8,24},{9,... | collective-permute-start | bytes 294920 | tf_op jit(solution)/shard_map/ppermute | solution.py:447
  65.6 7.2 %collective-permute-start.9 = (bf16[16,768]{1,0:T(8,128)(2,1)S(1)}, bf16[16,768]{1,0:T(8,128)(2,1)S(1)}, u32[]{:S(2)}, u32[]{:S(2)}) collective-permute-start(bf16[16,768]{1,0:T(8,128)(2,1)S(1)} %get-tuple-element.77), channel_id=1, source_target_pairs={{0,1},{1,2},{2,3},{3,0},{4,5},{5,6},{6,7},{7,4},{8,9},{9,10},{10,1... | collective-permute-start | bytes 73736 | tf_op jit(solution)/shard_map/ppermute | solution.py:447
  66.2 9.2 %collective-permute-start.10 = (bf16[16,768]{1,0:T(8,128)(2,1)S(1)}, bf16[16,768]{1,0:T(8,128)(2,1)S(1)}, u32[]{:S(2)}, u32[]{:S(2)}) collective-permute-start(bf16[16,768]{1,0:T(8,128)(2,1)S(1)} %get-tuple-element.78), channel_id=1, source_target_pairs={{0,2},{1,3},{2,0},{3,1},{4,6},{5,7},{6,4},{7,5},{8,10},{9,11},{10,... | collective-permute-start | bytes 73736 | tf_op jit(solution)/shard_map/ppermute | solution.py:447
  68.4 7.0 %collective-permute-start.11 = (bf16[16,768]{1,0:T(8,128)(2,1)S(1)}, bf16[16,768]{1,0:T(8,128)(2,1)S(1)}, u32[]{:S(2)}, u32[]{:S(2)}) collective-permute-start(bf16[16,768]{1,0:T(8,128)(2,1)S(1)} %get-tuple-element.79), channel_id=1, source_target_pairs={{0,3},{1,0},{2,1},{3,2},{4,7},{5,4},{6,5},{7,6},{8,11},{9,8},{10,9... | collective-permute-start | bytes 73736 | tf_op jit(solution)/shard_map/ppermute | solution.py:447
  70.6 11.2 %collective-permute-start.6 = (bf16[96,1536]{1,0:T(8,128)(2,1)S(1)}, bf16[96,1536]{1,0:T(8,128)(2,1)S(1)}, u32[]{:S(2)}, u32[]{:S(2)}) collective-permute-start(bf16[96,1536]{1,0:T(8,128)(2,1)S(1)} %get-tuple-element.85), channel_id=1, source_target_pairs={{0,1},{1,2},{2,3},{3,0},{4,5},{5,6},{6,7},{7,4},{8,9},{9,10},{10,1... | collective-permute-start | bytes 884744 | tf_op jit(solution)/shard_map/ppermute | solution.py:447
  71.3 10.4 %collective-permute-start.7 = (bf16[96,1536]{1,0:T(8,128)(2,1)S(1)}, bf16[96,1536]{1,0:T(8,128)(2,1)S(1)}, u32[]{:S(2)}, u32[]{:S(2)}) collective-permute-start(bf16[96,1536]{1,0:T(8,128)(2,1)S(1)} %get-tuple-element.86), channel_id=1, source_target_pairs={{0,2},{1,3},{2,0},{3,1},{4,6},{5,7},{6,4},{7,5},{8,10},{9,11},{10,... | collective-permute-start | bytes 884744 | tf_op jit(solution)/shard_map/ppermute | solution.py:447
  72.8 9.8 %collective-permute-start.8 = (bf16[96,1536]{1,0:T(8,128)(2,1)S(1)}, bf16[96,1536]{1,0:T(8,128)(2,1)S(1)}, u32[]{:S(2)}, u32[]{:S(2)}) collective-permute-start(bf16[96,1536]{1,0:T(8,128)(2,1)S(1)} %get-tuple-element.87), channel_id=1, source_target_pairs={{0,3},{1,0},{2,1},{3,2},{4,7},{5,4},{6,5},{7,6},{8,11},{9,8},{10,9... | collective-permute-start | bytes 884744 | tf_op jit(solution)/shard_map/ppermute | solution.py:447
  82.9 6.9 %collective-permute-start.12 = (bf16[64,768]{1,0:T(8,128)(2,1)S(1)}, bf16[64,768]{1,0:T(8,128)(2,1)S(1)}, u32[]{:S(2)}, u32[]{:S(2)}) collective-permute-start(bf16[64,768]{1,0:T(8,128)(2,1)S(1)} %get-tuple-element.93), channel_id=1, source_target_pairs={{0,4},{1,5},{2,6},{3,7},{4,8},{5,9},{6,10},{7,11},{8,12},{9,13},{1... | collective-permute-start | bytes 294920 | tf_op jit(solution)/shard_map/ppermute | solution.py:447
  83.5 6.4 %collective-permute-start.13 = (bf16[64,768]{1,0:T(8,128)(2,1)S(1)}, bf16[64,768]{1,0:T(8,128)(2,1)S(1)}, u32[]{:S(2)}, u32[]{:S(2)}) collective-permute-start(bf16[64,768]{1,0:T(8,128)(2,1)S(1)} %get-tuple-element.94), channel_id=1, source_target_pairs={{0,8},{1,9},{2,10},{3,11},{4,12},{5,13},{6,14},{7,15},{8,0},{9,1},... | collective-permute-start | bytes 294920 | tf_op jit(solution)/shard_map/ppermute | solution.py:447
  85.5 5.2 %collective-permute-start.14 = (bf16[64,768]{1,0:T(8,128)(2,1)S(1)}, bf16[64,768]{1,0:T(8,128)(2,1)S(1)}, u32[]{:S(2)}, u32[]{:S(2)}) collective-permute-start(bf16[64,768]{1,0:T(8,128)(2,1)S(1)} %get-tuple-element.95), channel_id=1, source_target_pairs={{0,12},{1,13},{2,14},{3,15},{4,0},{5,1},{6,2},{7,3},{8,4},{9,5},{1... | collective-permute-start | bytes 294920 | tf_op jit(solution)/shard_map/ppermute | solution.py:447

commit v3 on v2

--- a/solution.py
+++ b/solution.py
@@ -480,11 +480,11 @@
     rows_out = embed_rows(send_table, map_mean, emb, other_emb)
     payloads, _ = lax.optimization_barrier((payloads, rows_out))
     *pays, own = combine(payloads, units)
-    received = [move(pays[hop - 1], 2, hop) for hop in (1, 2, 3)]
+    received = [move(pays[hop - 1], 2, hop) for hop in (1, 3, 2)]
     moved = [move(rows_out[hop], 4, hop) for hop in (1, 2, 3)]
     own_embed, *embeds = regroup_rows((rows_out[0], *moved))
     own, *pays = second_sum(own, received, embeds)
-    by_hop = {hop: move(pays[hop - 1], 3, hop) for hop in (1, 2, 3)}
+    by_hop = {hop: move(pays[hop - 1], 3, hop) for hop in (1, 3, 2)}
     up_part, down_part, arrived = last_sum(
         place, own, own_embed, [by_hop[hop] for hop in (1, 2, 3)]
     )

time: 91.7 us -> 91.2 us (level)
  transfers between devices with their start and end apart: 15 -> 15, of which waited for: 6 -> 7; matrix products, arithmetic and copies ran while one was open for 0% -> 0% of each run, Pallas kernels for 19% -> 19%
where the time goes in v3:
time: 91.2 us; the launch traced here: 91 us
  Pallas kernels  39.1 us (43%)
  starting transfers between devices  19.4 us (21%)
  blocking collectives  15.7 us (17%)
  waiting for transfers between devices  13.6 us (15%)
  local copies, waits for them, and re-layouts  2.28 us (2%)
    pallas_call x4, Pallas kernels, hidden_block(): pl.pallas_call(block_kernel, out_shape=(jax.ShapeDtypeStruct((units + 3 *...  21.8 us
    ppermute x15, starting transfers between devices, move(): return lax.ppermute(value, axes, pairs)  19.4 us
    all_to_all x1, blocking collectives, body(): lax.all_to_all(jnp.transpose(embed_grad[0, 0], (1, 0, 2)), 'enc', split_a...  15.7 us
    pallas_call x1, Pallas kernels, conv_norm(): pl.pallas_call(conv_kernel, out_shape=(shape((cells, tiles, width), jnp.b...  15.1 us
    ppermute x15, waiting for transfers between devices, move(): return lax.ppermute(value, axes, pairs)  13.6 us
    unnamed x9, local copies, waits for them, and re-layouts  2.25 us
  transfers between devices with their start and end apart: 15, of which 7 were waited for; matrix products, arithmetic and copies ran while one was open for 0% of the time, Pallas kernels for 19%

profile of v3, /device:TPU:0, one launch (start us, length us, event | category | flops | bytes accessed | tf_op | source)
XLA Modules:
  0.0 91.0 jit_solution(5953673524847642056)
XLA Ops:
  0.6 0.0 copy-start
  0.6 0.9 copy-done
  1.5 0.7 copy-done.1
  2.2 0.7 copy-done.2
  2.8 15.1 %conv_norm.1 = (bf16[49,32,768]{2,1,0:T(8,128)(2,1)S(1)}, f32[32,768]{1,0:T(8,128)S(1)}, bf16[32,48]{1,0:T(8,128)(2,1)S(1)}, bf16[32,64]{1,0:T(8,128)(2,1)S(1)},...) custom-call(s32[1,16]{1,0:T(1,128)S(1)} %copy-done.1, ...), custom_call_target="tpu_custom_call" | custom-call | flops 1000 | bytes 1000 | tf_op jit(solution)/shard_map/conv_norm/pallas_call | solution.py:142
  18.0 0.1 collective-permute-start
  18.1 0.0 copy-done.3
  18.1 0.1 copy.14
  18.1 15.7 %all_to_all.5 = bf16[3,16,768]{2,0,1:T(4,128)(2,1)S(1)} all-to-all(bf16[3,16,768]{2,0,1:T(4,128)(2,1)S(1)} %bitcast.25), channel_id=1, replica_groups=mesh['slide'=8,'enc'=16] {'enc'}, dimensions={1} | all-to-all | bytes 147456 | tf_op jit(solution)/shard_map/all_to_all | solution.py:457
  33.8 0.1 convolution_convert_fusion.rest_2_
  34.0 0.1 collective-permute-start.1
  34.1 1.2 %collective-permute-done.1.rest_3_ = bf16[32,768]{1,0:T(8,128)(2,1)S(1)} collective-permute-done((bf16[32,768]{1,0:T(8,128)(2,1)S(1)}, bf16[32,768]{1,0:T(8,128)(2,1)S(1)}, u32[]{:S(2)}, u32[]{:S(2)}) %collective-permute-start.1) | collective-permute-done | bytes 49184 | tf_op jit(solution)/shard_map/ppermute | solution.py:447
  35.3 0.0 collective-permute-done.rest_1_
  35.3 5.4 %hidden_block.4 = (bf16[480,768]{1,0:T(8,128)(2,1)S(1)}, f32[64,768]{1,0:T(8,128)S(1)}) custom-call(bf16[1568,768]{1,0:T(8,128)(2,1)S(1)} %bitcast.19, bf16[1568,768]{1,0:T(8,128)(2,1)S(1)} %collective-permute-done.rest_1_, bf16[32,768]{1,0:T(8,128)(2,1)S(1)} %convolution_convert_fusion.rest_2_, bf16[32,768]{1,0:T(8,128)(2,1)S(1)} %collective-permute-done.1.rest_3_, ...), custom_call_target="tpu_custom_call" | custom-call | flops 1000 | bytes 1000 | tf_op jit(solution)/shard_map/hidden_block/pallas_call | solution.py:256
  40.8 3.3 %collective-permute-start.2 = (bf16[480,768]{1,0:T(8,128)(2,1)S(1)}, bf16[480,768]{1,0:T(8,128)(2,1)S(1)}, u32[]{:S(2)}, u32[]{:S(2)}) collective-permute-start(bf16[480,768]{1,0:T(8,128)(2,1)S(1)} %get-tuple-element.63), channel_id=1, source_target_pairs={{0,64},{1,65},{2,66},{3,67},{4,68},{5,69},{6,70},{7,71},{8,72},{9,... | collective-permute-start | bytes 2211848 | tf_op jit(solution)/shard_map/ppermute | solution.py:447
  44.0 5.4 %hidden_block.5 = (bf16[480,768]{1,0:T(8,128)(2,1)S(1)}, f32[64,768]{1,0:T(8,128)S(1)}) custom-call(bf16[1568,768]{1,0:T(8,128)(2,1)S(1)} %bitcast.20, bf16[1568,768]{1,0:T(8,128)(2,1)S(1)} %collective-permute-done.rest_1_, bf16[32,768]{1,0:T(8,128)(2,1)S(1)} %convolution_convert_fusion.rest_2_, bf16[32,768]{1,0:T(8,128)(2,1)S(1)} %collective-permute-done.1.rest_3_, ...), custom_call_target="tpu_custom_call" | custom-call | flops 1000 | bytes 1000 | tf_op jit(solution)/shard_map/hidden_block/pallas_call | solution.py:256
  49.5 0.7 collective-permute-start.3
  50.2 5.4 %hidden_block.6 = (bf16[480,768]{1,0:T(8,128)(2,1)S(1)}, f32[64,768]{1,0:T(8,128)S(1)}) custom-call(bf16[1568,768]{1,0:T(8,128)(2,1)S(1)} %bitcast.21, bf16[1568,768]{1,0:T(8,128)(2,1)S(1)} %collective-permute-done.rest_1_, bf16[32,768]{1,0:T(8,128)(2,1)S(1)} %convolution_convert_fusion.rest_2_, bf16[32,768]{1,0:T(8,128)(2,1)S(1)} %collective-permute-done.1.rest_3_, ...), custom_call_target="tpu_custom_call" | custom-call | flops 1000 | bytes 1000 | tf_op jit(solution)/shard_map/hidden_block/pallas_call | solution.py:256
  55.6 2.9 %collective-permute-start.5 = (bf16[480,768]{1,0:T(8,128)(2,1)S(1)}, bf16[480,768]{1,0:T(8,128)(2,1)S(1)}, u32[]{:S(2)}, u32[]{:S(2)}) collective-permute-start(bf16[480,768]{1,0:T(8,128)(2,1)S(1)} %get-tuple-element.71), channel_id=1, source_target_pairs={{0,96},{1,97},{2,98},{3,99},{4,100},{5,101},{6,102},{7,103},{8,104... | collective-permute-start | bytes 2211848 | tf_op jit(solution)/shard_map/ppermute | solution.py:447
  58.5 0.0 collective-permute-done.2.a_ref
  58.5 5.4 %hidden_block.7 = (bf16[480,768]{1,0:T(8,128)(2,1)S(1)}, f32[64,768]{1,0:T(8,128)S(1)}) custom-call(bf16[1568,768]{1,0:T(8,128)(2,1)S(1)} %bitcast.22, bf16[1568,768]{1,0:T(8,128)(2,1)S(1)} %collective-permute-done.rest_1_, bf16[32,768]{1,0:T(8,128)(2,1)S(1)} %convolution_convert_fusion.rest_2_, bf16[32,768]{1,0:T(8,128)(2,1)S(1)} %collective-permute-done.1.rest_3_, ...), custom_call_target="tpu_custom_call" | custom-call | flops 1000 | bytes 1000 | tf_op jit(solution)/shard_map/hidden_block/pallas_call | solution.py:256
  64.0 0.1 collective-permute-start.4
  64.1 0.0 collective-permute-done.3.b_ref
  64.1 1.3 %collective-permute-done.4.other_ref = f32[32,768]{1,0:T(8,128)S(1)} collective-permute-done((f32[32,768]{1,0:T(8,128)S(1)}, f32[32,768]{1,0:T(8,128)S(1)}, u32[]{:S(2)}, u32[]{:S(2)}) %collective-permute-start.4) | collective-permute-done | bytes 98336 | tf_op jit(solution)/shard_map/ppermute | solution.py:447
  65.4 0.2 embed_rows.1
  65.6 0.6 collective-permute-start.9
  66.2 2.2 %collective-permute-start.10 = (bf16[16,768]{1,0:T(8,128)(2,1)S(1)}, bf16[16,768]{1,0:T(8,128)(2,1)S(1)}, u32[]{:S(2)}, u32[]{:S(2)}) collective-permute-start(bf16[16,768]{1,0:T(8,128)(2,1)S(1)} %get-tuple-element.78), channel_id=1, source_target_pairs={{0,2},{1,3},{2,0},{3,1},{4,6},{5,7},{6,4},{7,5},{8,10},{9,11},{10,... | collective-permute-start | bytes 73736 | tf_op jit(solution)/shard_map/ppermute | solution.py:447
  68.4 1.4 %collective-permute-start.11 = (bf16[16,768]{1,0:T(8,128)(2,1)S(1)}, bf16[16,768]{1,0:T(8,128)(2,1)S(1)}, u32[]{:S(2)}, u32[]{:S(2)}) collective-permute-start(bf16[16,768]{1,0:T(8,128)(2,1)S(1)} %get-tuple-element.79), channel_id=1, source_target_pairs={{0,3},{1,0},{2,1},{3,2},{4,7},{5,4},{6,5},{7,6},{8,11},{9,8},{10,9... | collective-permute-start | bytes 73736 | tf_op jit(solution)/shard_map/ppermute | solution.py:447
  69.7 0.0 collective-permute-done.5.c_ref
  69.8 0.8 combine.1
  70.6 0.7 collective-permute-start.6
  71.3 2.6 %collective-permute-start.7 = (bf16[96,1536]{1,0:T(8,128)(2,1)S(1)}, bf16[96,1536]{1,0:T(8,128)(2,1)S(1)}, u32[]{:S(2)}, u32[]{:S(2)}) collective-permute-start(bf16[96,1536]{1,0:T(8,128)(2,1)S(1)} %get-tuple-element.86), channel_id=1, source_target_pairs={{0,3},{1,0},{2,1},{3,2},{4,7},{5,4},{6,5},{7,6},{8,11},{9,8},{10,9... | collective-permute-start | bytes 884744 | tf_op jit(solution)/shard_map/ppermute | solution.py:447
  73.9 0.0 collective-permute-done.9.refs_1_
  73.9 0.8 collective-permute-start.8
  74.7 0.0 collective-permute-done.10.refs_2_
  74.7 0.0 collective-permute-done.11.refs_3_
  74.7 0.2 regroup_rows.1
  74.9 3.7 %collective-permute-done.6.rest_0_ = bf16[96,1536]{1,0:T(8,128)(2,1)S(1)} collective-permute-done((bf16[96,1536]{1,0:T(8,128)(2,1)S(1)}, bf16[96,1536]{1,0:T(8,128)(2,1)S(1)}, u32[]{:S(2)}, u32[]{:S(2)}) %collective-permute-start.6) | collective-permute-done | bytes 294944 | tf_op jit(solution)/shard_map/ppermute | solution.py:447
  78.6 2.7 %collective-permute-done.7.rest_1_ = bf16[96,1536]{1,0:T(8,128)(2,1)S(1)} collective-permute-done((bf16[96,1536]{1,0:T(8,128)(2,1)S(1)}, bf16[96,1536]{1,0:T(8,128)(2,1)S(1)}, u32[]{:S(2)}, u32[]{:S(2)}) %collective-permute-start.7) | collective-permute-done | bytes 294944 | tf_op jit(solution)/shard_map/ppermute | solution.py:447
  81.3 0.8 collective-permute-done.8.rest_2_
  82.1 0.3 second_sum.1
  82.4 0.6 collective-permute-start.12
  82.9 2.1 %collective-permute-start.13 = (bf16[64,768]{1,0:T(8,128)(2,1)S(1)}, bf16[64,768]{1,0:T(8,128)(2,1)S(1)}, u32[]{:S(2)}, u32[]{:S(2)}) collective-permute-start(bf16[64,768]{1,0:T(8,128)(2,1)S(1)} %get-tuple-element.94), channel_id=1, source_target_pairs={{0,8},{1,9},{2,10},{3,11},{4,12},{5,13},{6,14},{7,15},{8,0},{9,1},... | collective-permute-start | bytes 294920 | tf_op jit(solution)/shard_map/ppermute | solution.py:447
  85.0 1.3 %collective-permute-start.14 = (bf16[64,768]{1,0:T(8,128)(2,1)S(1)}, bf16[64,768]{1,0:T(8,128)(2,1)S(1)}, u32[]{:S(2)}, u32[]{:S(2)}) collective-permute-start(bf16[64,768]{1,0:T(8,128)(2,1)S(1)} %get-tuple-element.95), channel_id=1, source_target_pairs={{0,12},{1,13},{2,14},{3,15},{4,0},{5,1},{6,2},{7,3},{8,4},{9,5},{1... | collective-permute-start | bytes 294920 | tf_op jit(solution)/shard_map/ppermute | solution.py:447
  86.3 3.0 %collective-permute-done.12.a_ref = bf16[64,768]{1,0:T(8,128)(2,1)S(1)} collective-permute-done((bf16[64,768]{1,0:T(8,128)(2,1)S(1)}, bf16[64,768]{1,0:T(8,128)(2,1)S(1)}, u32[]{:S(2)}, u32[]{:S(2)}) %collective-permute-start.12) | collective-permute-done | bytes 98336 | tf_op jit(solution)/shard_map/ppermute | solution.py:447
  89.3 0.0 collective-permute-done.13.b_ref
  89.3 0.9 collective-permute-done.14.c_ref
  90.2 0.8 last_sum.1
  (6 shorter events, 0.0 us)
Async XLA Ops:
  0.6 0.9 copy-start
  1.5 0.7 copy-start.1
  2.2 0.7 copy-start.2
  2.8 15.2 %copy-start.3 = (bf16[1,1,16,3,768]{4,2,3,1,0:T(8,128)(2,1)S(1)}, bf16[1,1,16,3,768]{4,2,3,1,0:T(8,128)(2,1)}, u32[]{:S(2)}) copy-start(bf16[1,1,16,3,768]{4,2,3,1,0:T(8,128)(2,1)} %param.10) | copy-start | bytes 221188
  18.0 17.3 %collective-permute-start = (bf16[1568,768]{1,0:T(8,128)(2,1)S(1)}, bf16[1568,768]{1,0:T(8,128)(2,1)S(1)}, u32[]{:S(2)}, u32[]{:S(2)}) collective-permute-start(bf16[1568,768]{1,0:T(8,128)(2,1)S(1)} %bitcast.18), channel_id=1, source_target_pairs={{0,16},{1,17},{2,18},{3,19},{4,20},{5,21},{6,22},{7,23},{8,24},{9,... | collective-permute-start | bytes 7225352 | tf_op jit(solution)/shard_map/ppermute | solution.py:447
  34.0 1.3 %collective-permute-start.1 = (bf16[32,768]{1,0:T(8,128)(2,1)S(1)}, bf16[32,768]{1,0:T(8,128)(2,1)S(1)}, u32[]{:S(2)}, u32[]{:S(2)}) collective-permute-start(bf16[32,768]{1,0:T(8,128)(2,1)S(1)} %convolution_convert_fusion.rest_2_), channel_id=1, source_target_pairs={{0,16},{1,17},{2,18},{3,19},{4,20},{5,21},{6,22},{7,23},{8,24},{9,... | collective-permute-start | bytes 147464 | tf_op jit(solution)/shard_map/ppermute | solution.py:447
  40.8 17.8 %collective-permute-start.2 = (bf16[480,768]{1,0:T(8,128)(2,1)S(1)}, bf16[480,768]{1,0:T(8,128)(2,1)S(1)}, u32[]{:S(2)}, u32[]{:S(2)}) collective-permute-start(bf16[480,768]{1,0:T(8,128)(2,1)S(1)} %get-tuple-element.63), channel_id=1, source_target_pairs={{0,64},{1,65},{2,66},{3,67},{4,68},{5,69},{6,70},{7,71},{8,72},{9,... | collective-permute-start | bytes 2211848 | tf_op jit(solution)/shard_map/ppermute | solution.py:447
  49.5 14.6 %collective-permute-start.3 = (bf16[480,768]{1,0:T(8,128)(2,1)S(1)}, bf16[480,768]{1,0:T(8,128)(2,1)S(1)}, u32[]{:S(2)}, u32[]{:S(2)}) collective-permute-start(bf16[480,768]{1,0:T(8,128)(2,1)S(1)} %get-tuple-element.65), channel_id=1, source_target_pairs={{0,32},{1,33},{2,34},{3,35},{4,36},{5,37},{6,38},{7,39},{8,40},{9,... | collective-permute-start | bytes 2211848 | tf_op jit(solution)/shard_map/ppermute | solution.py:447
  55.6 14.2 %collective-permute-start.5 = (bf16[480,768]{1,0:T(8,128)(2,1)S(1)}, bf16[480,768]{1,0:T(8,128)(2,1)S(1)}, u32[]{:S(2)}, u32[]{:S(2)}) collective-permute-start(bf16[480,768]{1,0:T(8,128)(2,1)S(1)} %get-tuple-element.71), channel_id=1, source_target_pairs={{0,96},{1,97},{2,98},{3,99},{4,100},{5,101},{6,102},{7,103},{8,104... | collective-permute-start | bytes 2211848 | tf_op jit(solution)/shard_map/ppermute | solution.py:447
  64.0 1.4 %collective-permute-start.4 = (f32[32,768]{1,0:T(8,128)S(1)}, f32[32,768]{1,0:T(8,128)S(1)}, u32[]{:S(2)}, u32[]{:S(2)}) collective-permute-start(f32[32,768]{1,0:T(8,128)S(1)} %slice.3), channel_id=1, source_target_pairs={{0,16},{1,17},{2,18},{3,19},{4,20},{5,21},{6,22},{7,23},{8,24},{9,... | collective-permute-start | bytes 294920 | tf_op jit(solution)/shard_map/ppermute | solution.py:447
  65.6 8.3 %collective-permute-start.9 = (bf16[16,768]{1,0:T(8,128)(2,1)S(1)}, bf16[16,768]{1,0:T(8,128)(2,1)S(1)}, u32[]{:S(2)}, u32[]{:S(2)}) collective-permute-start(bf16[16,768]{1,0:T(8,128)(2,1)S(1)} %get-tuple-element.77), channel_id=1, source_target_pairs={{0,1},{1,2},{2,3},{3,0},{4,5},{5,6},{6,7},{7,4},{8,9},{9,10},{10,1... | collective-permute-start | bytes 73736 | tf_op jit(solution)/shard_map/ppermute | solution.py:447
  66.2 8.6 %collective-permute-start.10 = (bf16[16,768]{1,0:T(8,128)(2,1)S(1)}, bf16[16,768]{1,0:T(8,128)(2,1)S(1)}, u32[]{:S(2)}, u32[]{:S(2)}) collective-permute-start(bf16[16,768]{1,0:T(8,128)(2,1)S(1)} %get-tuple-element.78), channel_id=1, source_target_pairs={{0,2},{1,3},{2,0},{3,1},{4,6},{5,7},{6,4},{7,5},{8,10},{9,11},{10,... | collective-permute-start | bytes 73736 | tf_op jit(solution)/shard_map/ppermute | solution.py:447
  68.4 6.4 %collective-permute-start.11 = (bf16[16,768]{1,0:T(8,128)(2,1)S(1)}, bf16[16,768]{1,0:T(8,128)(2,1)S(1)}, u32[]{:S(2)}, u32[]{:S(2)}) collective-permute-start(bf16[16,768]{1,0:T(8,128)(2,1)S(1)} %get-tuple-element.79), channel_id=1, source_target_pairs={{0,3},{1,0},{2,1},{3,2},{4,7},{5,4},{6,5},{7,6},{8,11},{9,8},{10,9... | collective-permute-start | bytes 73736 | tf_op jit(solution)/shard_map/ppermute | solution.py:447
  70.6 8.0 %collective-permute-start.6 = (bf16[96,1536]{1,0:T(8,128)(2,1)S(1)}, bf16[96,1536]{1,0:T(8,128)(2,1)S(1)}, u32[]{:S(2)}, u32[]{:S(2)}) collective-permute-start(bf16[96,1536]{1,0:T(8,128)(2,1)S(1)} %get-tuple-element.85), channel_id=1, source_target_pairs={{0,1},{1,2},{2,3},{3,0},{4,5},{5,6},{6,7},{7,4},{8,9},{9,10},{10,1... | collective-permute-start | bytes 884744 | tf_op jit(solution)/shard_map/ppermute | solution.py:447
  71.3 10.0 %collective-permute-start.7 = (bf16[96,1536]{1,0:T(8,128)(2,1)S(1)}, bf16[96,1536]{1,0:T(8,128)(2,1)S(1)}, u32[]{:S(2)}, u32[]{:S(2)}) collective-permute-start(bf16[96,1536]{1,0:T(8,128)(2,1)S(1)} %get-tuple-element.86), channel_id=1, source_target_pairs={{0,3},{1,0},{2,1},{3,2},{4,7},{5,4},{6,5},{7,6},{8,11},{9,8},{10,9... | collective-permute-start | bytes 884744 | tf_op jit(solution)/shard_map/ppermute | solution.py:447
  73.9 8.2 %collective-permute-start.8 = (bf16[96,1536]{1,0:T(8,128)(2,1)S(1)}, bf16[96,1536]{1,0:T(8,128)(2,1)S(1)}, u32[]{:S(2)}, u32[]{:S(2)}) collective-permute-start(bf16[96,1536]{1,0:T(8,128)(2,1)S(1)} %get-tuple-element.87), channel_id=1, source_target_pairs={{0,2},{1,3},{2,0},{3,1},{4,6},{5,7},{6,4},{7,5},{8,10},{9,11},{10,... | collective-permute-start | bytes 884744 | tf_op jit(solution)/shard_map/ppermute | solution.py:447
  82.4 6.9 %collective-permute-start.12 = (bf16[64,768]{1,0:T(8,128)(2,1)S(1)}, bf16[64,768]{1,0:T(8,128)(2,1)S(1)}, u32[]{:S(2)}, u32[]{:S(2)}) collective-permute-start(bf16[64,768]{1,0:T(8,128)(2,1)S(1)} %get-tuple-element.93), channel_id=1, source_target_pairs={{0,4},{1,5},{2,6},{3,7},{4,8},{5,9},{6,10},{7,11},{8,12},{9,13},{1... | collective-permute-start | bytes 294920 | tf_op jit(solution)/shard_map/ppermute | solution.py:447
  82.9 6.4 %collective-permute-start.13 = (bf16[64,768]{1,0:T(8,128)(2,1)S(1)}, bf16[64,768]{1,0:T(8,128)(2,1)S(1)}, u32[]{:S(2)}, u32[]{:S(2)}) collective-permute-start(bf16[64,768]{1,0:T(8,128)(2,1)S(1)} %get-tuple-element.94), channel_id=1, source_target_pairs={{0,8},{1,9},{2,10},{3,11},{4,12},{5,13},{6,14},{7,15},{8,0},{9,1},... | collective-permute-start | bytes 294920 | tf_op jit(solution)/shard_map/ppermute | solution.py:447
  85.0 5.2 %collective-permute-start.14 = (bf16[64,768]{1,0:T(8,128)(2,1)S(1)}, bf16[64,768]{1,0:T(8,128)(2,1)S(1)}, u32[]{:S(2)}, u32[]{:S(2)}) collective-permute-start(bf16[64,768]{1,0:T(8,128)(2,1)S(1)} %get-tuple-element.95), channel_id=1, source_target_pairs={{0,12},{1,13},{2,14},{3,15},{4,0},{5,1},{6,2},{7,3},{8,4},{9,5},{1... | collective-permute-start | bytes 294920 | tf_op jit(solution)/shard_map/ppermute | solution.py:447
